TPU v7x, 256 devices: a whole 4x4x8 slice. The times are simulated.
256 devices in a mesh: fsdp: 64 (over y_hi, z, x), tp: 4 (over y_lo, core).
Axes of the slice: x: 4, y: 4 (y_hi: 2, y_lo: 2; y = y_hi * 2 + y_lo), z: 8, core: 2. Of those that a mesh axis runs over, the one named last changes fastest.
Arguments:
- latents: bfloat16 [32768, 3072], P(('fsdp', 'tp')), may hold values from -6 to 6
- noise: bfloat16 [32768, 3072], P(('fsdp', 'tp')), may hold values from -6 to 6, as said below
- timestep: int32 [32], replicated, may hold values from 0 to 999
- winner: int32 [32], replicated, may hold values from 0 to 1
- norm_gain: float32 [3072], replicated, may hold values from 0.5 to 1.5
- reference_weight: bfloat16 [3072, 3072], P('tp'), may hold values from -1 to 1
- policy_master: float32 [3072, 3072], P('fsdp', 'tp'), may hold values from -1 to 1
- moment_first: float32 [3072, 3072], P('fsdp', 'tp'), may hold values from -0.06 to 0.06
- moment_second: float32 [3072, 3072], P('fsdp', 'tp'), may hold values from 1e-05 to 0.001
Outputs:
- new_master: float32 [3072, 3072], P('fsdp', 'tp')
- new_first: float32 [3072, 3072], P('fsdp', 'tp')
- new_second: float32 [3072, 3072], P('fsdp', 'tp')
- loss: float32 [], replicated
Inputs may be any that keep to these rules, and one draw needn't show every extreme that they name: The two images of a pair have equal noise, row for row.
All inputs are finite; a program needn't handle non-finite values.
Results may differ from a plain program's by a relative error of at most 0.0049.
Values may be sent and summed in bfloat16 or wider, within the bound.
No kernel may reach another device: no remote copies, remote signals or barrier semaphores. Data moves between devices by JAX's collectives and lax.ppermute only.
A program may use at most 128 MiB of HBM per device.

v0:
```python
import jax
import jax.numpy as jnp
from jax import lax
from jax.sharding import PartitionSpec as P

STEPS = 1000
ADAM_STEP = 100


BETA = 5000.0


def normalize(noisy, gain):
    mean_sq = jnp.mean(noisy * noisy, axis=1, keepdims=True)
    return jax.nn.gelu(noisy * lax.rsqrt(mean_sq + 1e-06) * gain, approximate=True).astype(
        jnp.bfloat16
    )


def preference(policy_error, reference_error, winner):
    gap = (policy_error - reference_error).reshape(-1, 2)
    first_wins = winner == 0
    gap_win = jnp.where(first_wins, gap[:, 0], gap[:, 1])
    gap_lose = jnp.where(first_wins, gap[:, 1], gap[:, 0])
    margin = -0.5 * BETA * (gap_win - gap_lose)
    loss = jnp.mean(jax.nn.softplus(-margin))
    weight = jax.nn.sigmoid(-margin) * BETA / (2.0 * gap.shape[0])
    first = jnp.where(first_wins, weight, -weight)
    return (loss, jnp.stack([first, -first], axis=1).reshape(-1))


def adam_update(master, first, second, gradient):
    new_first = 0.9 * first + 0.1 * gradient
    new_second = 0.999 * second + 0.001 * gradient * gradient
    first_hat = new_first / (1.0 - 0.9**ADAM_STEP)
    second_hat = new_second / (1.0 - 0.999**ADAM_STEP)
    new_master = master - 0.001 * (first_hat / (jnp.sqrt(second_hat) + 1e-08) + 0.01 * master)
    return (new_master, new_first, new_second)


def seq_table(first_row, rows, count_seq, seq_len):
    ids = (first_row + jnp.arange(rows, dtype=jnp.int32)) // seq_len
    return (ids[:, None] == jnp.arange(count_seq, dtype=jnp.int32)[None, :]).astype(jnp.float32)


def row_values(table, values):
    return jnp.dot(table, values, precision=lax.Precision.HIGHEST)


def noisy_pair(clean_bf, drawn_bf, moment):
    clean = clean_bf.astype(jnp.float32)
    drawn = drawn_bf.astype(jnp.float32)
    return ((1.0 - moment) * clean + moment * drawn, drawn - clean)


def body(
    latents,
    noise,
    timestep,
    winner,
    norm_gain,
    reference_weight,
    policy_master,
    moment_first,
    moment_second,
):
    tok, width = latents.shape
    n_tp = lax.axis_size("tp")
    tp_index = lax.axis_index("tp")
    fsdp_index = lax.axis_index("fsdp")
    count_seq = 2 * timestep.shape[0]
    group_rows = n_tp * tok
    seq_len = n_tp * tok
    block = width // n_tp
    group_start = fsdp_index * group_rows
    seq_times = jnp.repeat((timestep.astype(jnp.float32) + 0.5) / STEPS, 2)
    own_table = seq_table(group_start + tp_index * tok, tok, count_seq, seq_len)
    own_time = row_values(own_table, seq_times)[:, None]
    noisy, target = noisy_pair(latents, noise, own_time)
    features = normalize(noisy, norm_gain)
    group_feats = lax.all_gather(features, "tp", axis=0, tiled=True)
    policy_bf = policy_master.astype(jnp.bfloat16)
    columns = group_feats
    policy_cols = jnp.dot(
        columns,
        lax.all_gather(policy_bf, "fsdp", axis=0, tiled=True),
        preferred_element_type=jnp.float32,
    ).astype(jnp.bfloat16)
    noisy_here, target_here = (noisy, target)
    policy_here = lax.all_to_all(policy_cols, "tp", split_axis=0, concat_axis=1, tiled=True).astype(
        jnp.float32
    )
    my_feats = lax.dynamic_slice_in_dim(group_feats, tp_index * block, block, 1)
    total = lax.psum(jnp.dot(my_feats, reference_weight, preferred_element_type=jnp.float32), "tp")
    ref_here = lax.dynamic_slice_in_dim(total, tp_index * tok, tok, 0)
    base = noisy_here - target_here
    policy_diff = base + policy_here
    ref_diff = base + ref_here
    policy_rows_sq = jnp.sum(policy_diff * policy_diff, axis=1)
    ref_rows_sq = jnp.sum(ref_diff * ref_diff, axis=1)
    policy_sq, ref_sq = lax.psum(
        (
            jnp.dot(policy_rows_sq, own_table, precision=lax.Precision.HIGHEST),
            jnp.dot(ref_rows_sq, own_table, precision=lax.Precision.HIGHEST),
        ),
        ("fsdp", "tp"),
    )
    scale = float(seq_len * width)
    loss, coefficient = preference(policy_sq / scale, ref_sq / scale, winner)
    row_coef = row_values(own_table, coefficient)[:, None]
    velocity_grad = (row_coef * (2.0 / scale) * policy_diff).astype(jnp.bfloat16)
    grad_cols = lax.all_to_all(velocity_grad, "tp", split_axis=1, concat_axis=0, tiled=True)
    columns = group_feats
    gradient = lax.psum_scatter(
        lax.dot_general(
            columns, grad_cols, (((0,), (0,)), ((), ())), preferred_element_type=jnp.float32
        ),
        "fsdp",
        scatter_dimension=0,
        tiled=True,
    )
    new_master, new_first, new_second = adam_update(
        policy_master, moment_first, moment_second, gradient
    )
    return (new_master, new_first, new_second, loss)


def solution(mesh):
    return jax.shard_map(
        body,
        mesh=mesh,
        in_specs=(
            P(("fsdp", "tp"), None),
            P(("fsdp", "tp"), None),
            P(),
            P(),
            P(),
            P("tp", None),
            P("fsdp", "tp"),
            P("fsdp", "tp"),
            P("fsdp", "tp"),
        ),
        out_specs=(P("fsdp", "tp"), P("fsdp", "tp"), P("fsdp", "tp"), P()),
        check_vma=False,
    )
```

profile of v0, /device:TPU:2, one launch (start us, length us, event | category | flops | bytes accessed | tf_op | source)
XLA Modules:
  0.0 1245.5 jit_solution(2136224010691407115)
XLA Ops:
  7.3 0.8 add_multiply_fusion
  8.1 0.1 reshape.62
  8.2 0.2 broadcast_subtract_fusion
  8.4 1.9 multiply_reduce_fusion.2
  10.4 1.8 fusion.9
  12.3 0.6 convert_element_type.35
  13.1 42.3 %all-gather.3.cloned.1.call-done = bf16[512,3072]{1,0:T(8,128)(2,1)} async-done(((bf16[128,3072]{1,0:T(8,128)(2,1)}), bf16[512,3072]{1,0:T(8,128)(2,1)}) %all-gather.3.cloned.1.call-update) | async-done | bytes 3145744 | tf_op jit(solution)/shard_map/all_gather | solution.py:81
  55.4 7.9 fusion.12
  63.3 127.9 %all-gather.5.cloned.1.call-done = bf16[3072,768]{1,0:T(8,128)(2,1)} async-done(((bf16[48,768]{1,0:T(8,128)(2,1)}), bf16[3072,768]{1,0:T(8,128)(2,1)}) %all-gather.5.cloned.1.call-update) | async-done | bytes 4718608 | tf_op jit(solution)/shard_map/all_gather | solution.py:86
  191.2 6.8 convolution_convert_fusion
  198.0 3.5 all-to-all-start
  201.5 20.2 %all-to-all-done = bf16[4,128,768]{2,1,0:T(8,128)(2,1)S(1)} async-done(((bf16[4,128,768]{2,1,0:T(8,128)(2,1)}), bf16[4,128,768]{2,1,0:T(8,128)(2,1)S(1)}, u32[]{:S(2)}, u32[]{:S(2)}) %all-to-all-start) | async-done | bytes 786464 | tf_op jit(solution)/shard_map/all_to_all | solution.py:90
  221.7 0.1 convert_bitcast_fusion
  221.8 0.2 copy.21
  222.0 103.8 %all-reduce.3.cloned.1.call-done = f32[512,3072]{1,0:T(8,128)} async-done(((f32[512,3072]{1,0:T(8,128)}), f32[512,3072]{1,0:T(8,128)}) %all-reduce.3.cloned.1.call-update) | async-done | bytes 6291472 | tf_op jit(solution)/shard_map/psum | solution.py:94
  325.8 2.2 multiply_reduce_fusion.1
  328.0 0.2 convolution_bitcast_fusion.2
  328.2 0.2 convolution_bitcast_fusion.1
  328.4 76.0 %all-reduce = (f32[64]{0:T(128)S(1)}, f32[64]{0:T(128)S(1)}) all-reduce(f32[64]{0:T(128)S(1)} %convolution_bitcast_fusion.1, f32[64]{0:T(128)S(1)} %convolution_bitcast_fusion.2), channel_id=1, replica_groups=mesh['fsdp'=64,'tp'=4] {'fsdp','tp'}, use_global_device_ids=true, to_apply=%region_5.6 | all-reduce | flops 128 | bytes 1024 | tf_op jit(solution)/shard_map/psum | solution.py:101
  404.4 0.1 reshape.59
  404.5 0.2 slice_reduce_fusion.1
  404.7 0.6 fusion.19
  405.4 0.1 copy.18
  405.5 0.1 reshape.68
  405.6 0.2 fusion.10
  405.8 1.6 multiply_convert_fusion
  407.4 1.5 copy.19
  408.9 14.1 %all_to_all.32 = bf16[128,4,768]{0,2,1:T(8,128)(2,1)S(1)} all-to-all(bf16[128,4,768]{0,2,1:T(8,128)(2,1)S(1)} %bitcast.36), channel_id=1, replica_groups=mesh['fsdp'=64,'tp'=4] {'tp'}, dimensions={1} | all-to-all | bytes 1572864 | tf_op jit(solution)/shard_map/all_to_all | solution.py:112
  423.0 0.3 copy.20
  423.3 8.2 fusion.24
  432.1 804.0 %reduce-scatter.2.cloned.1.call-done = f32[48,768]{1,0:T(8,128)} async-done(((f32[3072,768]{1,0:T(8,128)}), f32[48,768]{1,0:T(8,128)}) %reduce-scatter.2.cloned.1.call-update) | async-done | bytes 147472 | tf_op jit(solution)/shard_map/reduce_scatter | solution.py:114
  1236.1 1.7 multiply_subtract_fusion
  (28 shorter events, 0.4 us)
Async XLA Ops:
  7.2 3.2 copy-start
  7.2 3.2 copy-start.1
  7.2 3.2 copy-start.5
  7.2 48.2 %all-gather.3.cloned.1.call-start = ((), (), s32[]{:S(2)}) async-start(), calls=%async_computation.3 | async-start | bytes 3932160 | tf_op jit(solution)/shard_map/all_gather | solution.py:81
  10.4 1.9 copy-start.2
  12.2 178.9 %all-gather.5.cloned.1.call-start = ((), (), s32[]{:S(2)}) async-start(), calls=%async_computation.4 | async-start | bytes 4792320 | tf_op jit(solution)/shard_map/all_gather | solution.py:86
  13.0 312.8 %all-reduce.3.cloned.1.call-start = ((), (), s32[]{:S(2)}) async-start(), calls=%async_computation.5 | async-start | bytes 12582912 | tf_op jit(solution)/shard_map/psum | solution.py:94
  198.0 23.7 %all-to-all-start = ((bf16[4,128,768]{2,1,0:T(8,128)(2,1)}), bf16[4,128,768]{2,1,0:T(8,128)(2,1)S(1)}, u32[]{:S(2)}, u32[]{:S(2)}) async-start(bf16[4,128,768]{2,1,0:T(8,128)(2,1)} %bitcast.1), calls=%async_computation | async-start | bytes 1572864 | tf_op jit(solution)/shard_map/all_to_all | solution.py:90
  201.5 1034.7 %reduce-scatter.2.cloned.1.call-start = ((), (), s32[]{:S(2)}) async-start(), calls=%async_computation.6 | async-start | bytes 9584640 | tf_op jit(solution)/shard_map/reduce_scatter | solution.py:114
  325.8 78.9 %copy-start.6 = (s32[32]{0:T(128)S(1)}, s32[32]{0:T(128)}, u32[]{:S(2)}) copy-start(s32[32]{0:T(128)} %param.12) | copy-start | bytes 388
  431.4 804.7 %copy-start.3 = (f32[48,768]{1,0:T(8,128)S(1)}, f32[48,768]{1,0:T(8,128)}, u32[]{:S(2)}) copy-start(f32[48,768]{1,0:T(8,128)} %param.16) | copy-start | bytes 442372
  431.4 804.7 %copy-start.4 = (f32[48,768]{1,0:T(8,128)S(1)}, f32[48,768]{1,0:T(8,128)}, u32[]{:S(2)}) copy-start(f32[48,768]{1,0:T(8,128)} %param.17) | copy-start | bytes 442372
Sparse Core Ops, SparseCore 0:
  12.4 42.9 all-gather.2
  59.6 131.5 all-gather.4
  193.9 131.8 all-reduce.2
  431.6 804.5 reduce-scatter.1
where the time goes:
time: 1250 us
  waiting for transfers between devices  1100 us (88%)
  blocking collectives  90.1 us (7%)
  matrix products  23.6 us (2%)
  between operations  15.8 us (1%)
    reduce_scatter x1, waiting for transfers between devices, body(): lax.psum_scatter(lax.dot_general(columns, grad_cols, (((0,), (0,)), ((),...  804 us
    all_gather x1, waiting for transfers between devices, body(): lax.all_gather(policy_bf, 'fsdp', axis=0, tiled=True)  128 us
    psum x1, waiting for transfers between devices, body(): lax.psum(jnp.dot(my_feats, reference_weight, preferred_element_type=jnp.f...  104 us
    psum x1, blocking collectives, body(): lax.psum((jnp.dot(policy_rows_sq, own_table, precision=lax.Precision.HIGH...  76 us
    all_gather x1, waiting for transfers between devices, body(): group_feats = lax.all_gather(features, 'tp', axis=0, tiled=True)  42.3 us
  transfers between devices with their start and end apart: 5, of which 5 were waited for; matrix products, arithmetic and copies ran while one was open for 1% of the time, Pallas kernels for 0%

commit v1 on v0

v1 whole, which is shorter than its diff:
```python
import jax
import jax.numpy as jnp
import numpy as np
from jax import lax
from jax.sharding import Mesh
from jax.sharding import PartitionSpec as P

STEPS = 1000
ADAM_STEP = 100
BETA = 5000.0
AXES = ("yh", "z", "xh", "xl", "yl", "c")
SIZES = (2, 8, 2, 2, 2, 2)
bf16 = jnp.bfloat16
f32 = jnp.float32


def normalize(noisy, gain):
    mean_sq = jnp.mean(noisy * noisy, axis=1, keepdims=True)
    return jax.nn.gelu(noisy * lax.rsqrt(mean_sq + 1e-06) * gain, approximate=True).astype(bf16)


def adam_update(master, first, second, gradient):
    new_first = 0.9 * first + 0.1 * gradient
    new_second = 0.999 * second + 0.001 * gradient * gradient
    first_hat = new_first / (1.0 - 0.9**ADAM_STEP)
    second_hat = new_second / (1.0 - 0.999**ADAM_STEP)
    new_master = master - 0.001 * (first_hat / (jnp.sqrt(second_hat) + 1e-08) + 0.01 * master)
    return (new_master, new_first, new_second)


def flip(x, *axes):
    last = 2 ** len(axes) - 1
    return lax.ppermute(x, axes, [(i, last - i) for i in range(last + 1)])


def ordered(index, own, other):
    return jnp.where(
        index == 0, jnp.concatenate([own, other]), jnp.concatenate([other, own])
    )


def body(
    latents, noise, timestep, winner, norm_gain, reference_weight, policy_master, moment_first, moment_second
):
    tok, width = latents.shape
    yh, z, xh, xl, yl, c = (lax.axis_index(a) for a in AXES)
    half = policy_master.shape[1] // 2
    pair = (yh * SIZES[1] + z) * SIZES[2] + xh
    count_pairs = timestep.shape[0]
    scale = float(4 * tok * width)
    time = (lax.dynamic_index_in_dim(timestep, pair, 0, False).astype(f32) + 0.5) / STEPS
    wins = lax.dynamic_index_in_dim(winner, pair, 0, False) == xl
    sign = jnp.where(wins, 1.0, -1.0).astype(f32)

    def columns(array, dx, dy, dc):
        block = ((yl ^ dy) * 2 + (c ^ dc)) * 2 + (xl ^ dx)
        return lax.dynamic_slice_in_dim(array, block * half, half, 1)

    policy_bf = policy_master.astype(bf16)
    own_w = lax.dynamic_slice_in_dim(policy_bf, xl * half, half, 1)
    other_w = flip(lax.dynamic_slice_in_dim(policy_bf, (1 - xl) * half, half, 1), "xl")
    policy_cols = lax.all_gather(ordered(xl, own_w, other_w), ("yh", "z", "xh"), axis=0, tiled=True)

    clean, drawn = latents.astype(f32), noise.astype(f32)
    feats = normalize((1.0 - time) * clean + time * drawn, norm_gain)
    h = tok // 2
    feats_y, feats_x = flip(feats, "yl"), flip(feats, "xl")
    feats_d = jnp.concatenate([flip(feats_y[:h], "xl"), flip(feats_x[h:], "yl")])
    group_feats = jnp.concatenate(
        [feats, feats_y, flip(feats, "c"), flip(feats_y, "c")]
        + [feats_x, feats_d, flip(feats_x, "c"), flip(feats_d, "c")]
    )

    def pack(dx, dy, dc, with_noise):
        parts = [columns(latents, dx, dy, dc)]
        return parts + ([columns(noise, dx, dy, dc)] if with_noise else [])

    got_y = flip(jnp.stack(pack(0, 1, 0, True) + pack(0, 1, 1, True)), "yl")
    got_x = flip(jnp.stack(pack(1, 0, 0, False) + pack(1, 0, 1, False)), "xl")
    got_d = flip(jnp.stack(pack(1, 1, 0, False) + pack(1, 1, 1, False)), "xl", "yl")
    swap = flip(
        jnp.concatenate([jnp.stack(pack(0, 0, 1, True)), got_y[2:], got_x[1:], got_d[1:]]), "c"
    )
    clean_own = jnp.concatenate([columns(latents, 0, 0, 0), got_y[0], swap[0], swap[2]])
    clean_other = jnp.concatenate([got_x[0], got_d[0], swap[4], swap[5]])
    drawn_cols = jnp.concatenate([columns(noise, 0, 0, 0), got_y[1], swap[1], swap[3]])
    clean_cols = jnp.stack([clean_own, clean_other]).astype(f32)
    drawn_cols = drawn_cols.astype(f32)[None]
    base = ((1.0 - time) * clean_cols + time * drawn_cols) - (drawn_cols - clean_cols)
    base = base.reshape(-1, half)
    signs = jnp.where(jnp.arange(base.shape[0])[:, None] < base.shape[0] // 2, sign, -sign)

    ref_c = flip(columns(reference_weight, 0, 0, 1), "c")
    ref_y = flip(columns(reference_weight, 0, 1, 0), "yh", "yl")
    ref_yc = flip(columns(reference_weight, 0, 1, 1), "yh", "yl", "c")
    ref_cols = ordered(
        yl, ordered(c, columns(reference_weight, 0, 0, 0), ref_c), ordered(c, ref_y, ref_yc)
    )

    policy_out = jnp.dot(group_feats, policy_cols, preferred_element_type=f32).astype(bf16).astype(f32)
    policy_diff = base + policy_out
    grad_cols = (signs * policy_diff).astype(bf16)
    partial = lax.dot_general(
        group_feats, grad_cols, (((0,), (0,)), ((), ())), preferred_element_type=f32
    ).astype(bf16)
    partial = partial.reshape(2, SIZES[1], 2, -1, half)

    def owned_by(dy, dx):
        block = lax.dynamic_index_in_dim(partial, yh ^ dy, 0, False)
        return lax.dynamic_index_in_dim(block, xh ^ dx, 1, False)

    got = [owned_by(0, 0), flip(owned_by(0, 1), "xh"), flip(owned_by(1, 0), "yh"), flip(owned_by(1, 1), "yh", "xh")]

    ref_diff = base + jnp.dot(group_feats, ref_cols, preferred_element_type=f32)
    gap = jnp.sum(signs * (policy_diff * policy_diff - ref_diff * ref_diff))
    gaps = lax.all_gather(gap, ("yh", "xh", "xl", "yl", "c")).reshape(2, 2, -1).sum(axis=2)
    margin = -0.5 * BETA * (gaps / scale)
    loss = jnp.sum(jax.nn.softplus(-margin))
    for step in (1, 2, 4):
        loss = loss + lax.ppermute(loss, "z", [(i, i ^ step) for i in range(SIZES[1])])
    loss = loss / count_pairs
    weight = jax.nn.sigmoid(-margin) * BETA / (2.0 * count_pairs) * (2.0 / scale)

    def weight_of(dy, dx):
        return weight[yh ^ dy, xh ^ dx]

    summed = (
        weight_of(0, 0) * got[0].astype(f32)
        + weight_of(0, 1) * got[1].astype(f32)
        + weight_of(1, 0) * got[2].astype(f32)
        + weight_of(1, 1) * got[3].astype(f32)
    ).astype(bf16)
    rows = policy_master.shape[0]
    blocks = lax.all_to_all(
        summed.reshape(-1, rows, half), ("z", "xl"), split_axis=0, concat_axis=0, tiled=True
    )
    blocks = blocks.reshape(SIZES[1], 2, rows, half).astype(f32).sum(axis=0)
    gradient = jnp.concatenate([blocks[0], blocks[1]], axis=1)
    return adam_update(policy_master, moment_first, moment_second, gradient) + (loss,)


def solution(mesh):
    fine = Mesh(mesh.devices.reshape(SIZES), AXES)
    fsdp, tp = AXES[:4], AXES[4:]
    return jax.shard_map(
        body,
        mesh=fine,
        in_specs=(P(AXES, None), P(AXES, None), P(), P(), P(), P(tp, None))
        + (P(fsdp, tp),) * 3,
        out_specs=(P(fsdp, tp), P(fsdp, tp), P(fsdp, tp), P()),
        check_vma=False,
    )
```

time: 1250 us -> 311 us (0.25)
  waiting for transfers between devices: 1100 us -> 125 us
  starting transfers between devices: 3.66 us -> 42.9 us
  blocking collectives: 90.1 us -> 58.8 us
  local copies, waits for them, and re-layouts: 2.63 us -> 25.2 us
    reduce_scatter x1 -> x0, waiting for transfers between devices: 804 us -> none  [body(): lax.psum_scatter(lax.dot_general(columns, grad_cols, (((0,), (0,)), ((),...]
    psum x1 -> x0, waiting for transfers between devices: 104 us -> none  [body(): lax.psum(jnp.dot(my_feats, reference_weight, preferred_element_type=jnp.f...]
    all_gather x2 -> x1, waiting for transfers between devices: 170 us -> 68.8 us  [body(): lax.all_gather(ordered(xl, own_w, other_w), ('yh', 'z', 'xh'), axis=0, ti...]
    psum x1 -> x0, blocking collectives: 76 us -> none  [body(): lax.psum((jnp.dot(policy_rows_sq, own_table, precision=lax.Precision.HIGH...]
    unnamed x0 -> x1, blocking collectives: none -> 58.8 us
    ppermute x0 -> x22, waiting for transfers between devices: none -> 55.9 us  [the longest x19 41 us: flip(): return lax.ppermute(x, axes, [(i, last - i) for i in range(last + 1)])]
    ppermute x0 -> x22, starting transfers between devices: none -> 28.3 us  [the longest x19 18.9 us: flip(): return lax.ppermute(x, axes, [(i, last - i) for i in range(last + 1)])]
    all_to_all x1, waiting for transfers between devices: 20.2 us -> 0.01 us  [body(): lax.all_to_all(summed.reshape(-1, rows, half), ('z', 'xl'), split_axis=0,...]
  transfers between devices with their start and end apart: 5 -> 24, of which waited for: 5 -> 10; matrix products, arithmetic and copies ran while one was open for 1% -> 12% of each run, Pallas kernels for 0% -> 0%
where the time goes in v1:
time: 311 us; the launch traced here: 310 us
  waiting for transfers between devices  125 us (40%)
  blocking collectives  58.8 us (19%)
  starting transfers between devices  42.9 us (14%)
  local copies, waits for them, and re-layouts  25.2 us (8%)
  matrix products  20.4 us (7%)
  between operations  19.3 us (6%)
  other arithmetic  18.5 us (6%)
    all_gather x1, waiting for transfers between devices, body(): lax.all_gather(ordered(xl, own_w, other_w), ('yh', 'z', 'xh'), axis=0, ti...  68.8 us
    unnamed x1, blocking collectives  58.8 us
    ppermute x19, waiting for transfers between devices, flip(): return lax.ppermute(x, axes, [(i, last - i) for i in range(last + 1)])  41 us
    ppermute x19, starting transfers between devices, flip(): return lax.ppermute(x, axes, [(i, last - i) for i in range(last + 1)])  18.9 us
    ppermute x3, waiting for transfers between devices, body(): lax.ppermute(loss, 'z', [(i, i ^ step) for i in range(SIZES[1])])  14.8 us
    all_to_all x1, starting transfers between devices, body(): lax.all_to_all(summed.reshape(-1, rows, half), ('z', 'xl'), split_axis=0,...  14.5 us
    unnamed x39, local copies, waits for them, and re-layouts  10.9 us
    ppermute x3, starting transfers between devices, body(): lax.ppermute(loss, 'z', [(i, i ^ step) for i in range(SIZES[1])])  9.44 us
  transfers between devices with their start and end apart: 24, of which 10 were waited for; matrix products, arithmetic and copies ran while one was open for 12% of the time, Pallas kernels for 0%

profile of v1, /device:TPU:2, one launch (start us, length us, event | category | flops | bytes accessed | tf_op | source)
XLA Modules:
  0.0 309.8 jit_solution(14940907549901912211)
XLA Ops:
  9.3 1.8 multiply_reduce_fusion
  11.1 2.0 constant_dynamic-update-slice_fusion.8
  13.1 1.6 collective-permute-start.4
  16.9 1.5 collective-permute-start.2
  26.4 2.9 constant_dynamic-slice_fusion.3
  29.9 9.2 %collective-permute-done.12 = bf16[48,384]{1,0:T(8,128)(2,1)} collective-permute-done((bf16[48,384]{1,0:T(8,128)(2,1)}, bf16[48,384]{1,0:T(8,128)(2,1)}, u32[]{:S(2)}, u32[]{:S(2)}) %collective-permute-start.12) | collective-permute-done | bytes 36896 | tf_op jit(solution)/shard_map/ppermute | solution.py:33
  39.6 1.5 maximum_select_fusion.6
  41.1 4.3 %collective-permute-done = bf16[4,128,384]{2,1,0:T(8,128)(2,1)} collective-permute-done((bf16[4,128,384]{2,1,0:T(8,128)(2,1)}, bf16[4,128,384]{2,1,0:T(8,128)(2,1)}, u32[]{:S(2)}, u32[]{:S(2)}) %collective-permute-start) | collective-permute-done | bytes 393248 | tf_op jit(solution)/shard_map/ppermute | solution.py:33
  45.4 1.6 collective-permute-start.15
  46.9 1.6 slice_dynamic-update-slice_fusion
  50.0 1.6 slice_bitcast_fusion.6
  51.7 1.6 slice_bitcast_fusion.5
  54.3 7.7 %collective-permute-done.15 = bf16[768,384]{1,0:T(8,128)(2,1)S(1)} collective-permute-done((bf16[768,384]{1,0:T(8,128)(2,1)S(1)}, bf16[768,384]{1,0:T(8,128)(2,1)S(1)}, u32[]{:S(2)}, u32[]{:S(2)}) %collective-permute-start.15) | collective-permute-done | bytes 589856 | tf_op jit(solution)/shard_map/ppermute | solution.py:33
  63.2 12.2 %collective-permute-done.14 = bf16[768,384]{1,0:T(8,128)(2,1)S(1)} collective-permute-done((bf16[768,384]{1,0:T(8,128)(2,1)}, bf16[768,384]{1,0:T(8,128)(2,1)S(1)}, u32[]{:S(2)}, u32[]{:S(2)}) %collective-permute-start.14) | collective-permute-done | bytes 589856 | tf_op jit(solution)/shard_map/ppermute | solution.py:33
  76.8 1.5 maximum_select_fusion.4
  82.5 7.4 %collective-permute-done.8 = bf16[64,3072]{1,0:T(8,128)(2,1)S(1)} collective-permute-done((bf16[64,3072]{1,0:T(8,128)(2,1)S(1)}, bf16[64,3072]{1,0:T(8,128)(2,1)S(1)}, u32[]{:S(2)}, u32[]{:S(2)}) %collective-permute-start.8) | collective-permute-done | bytes 393248 | tf_op jit(solution)/shard_map/ppermute | solution.py:33
  95.7 68.8 %all-gather.2.cloned.1.call-done = bf16[3072,384]{1,0:T(8,128)(2,1)} async-done(((bf16[96,384]{1,0:T(8,128)(2,1)}), bf16[3072,384]{1,0:T(8,128)(2,1)}) %all-gather.2.cloned.1.call-update) | async-done | bytes 2359312 | tf_op jit(solution)/shard_map/all_gather | solution.py:62
  164.4 6.9 %multiply_convert_fusion = (bf16[1024,384]{1,0:T(8,128)(2,1)S(1)}, bf16[1024,384]{1,0:T(8,128)(2,1)S(1)}) fusion(f32[2,512,384]{2,1,0:T(8,128)S(1)} %fusion.8, f32[1024]{0:T(1024)S(1)} %fusion.25, bf16[1024,3072]{1,0:T(8,128)(2,1)} %constant_dynamic-update-slice_fusion, bf16[3072,384]{1,0:T(8,128)(2,1)} %all-gather.2.cloned.1.call-done), kind=kOutput, calls=%fused_computation.28 | convolution fusion | flops 2417885184 | bytes 11800576 | tf_op jit(solution)/shard_map/dot_general | solution.py:100
  171.3 6.4 %convolution_convert_fusion = bf16[3072,384]{1,0:T(8,128)(2,1)S(1)} fusion(bf16[1024,3072]{1,0:T(8,128)(2,1)} %constant_dynamic-update-slice_fusion, bf16[1024,384]{1,0:T(8,128)(2,1)S(1)} %get-tuple-element.48), kind=kOutput, calls=%fused_computation | convolution fusion | flops 2417098752 | bytes 9437184 | tf_op jit(solution)/shard_map/dot_general | solution.py:103
  179.1 3.0 collective-permute-start.18
  182.1 2.1 collective-permute-start.17
  184.1 1.5 collective-permute-start.16
  185.6 7.1 %fusion.20 = f32[]{:T(128)} fusion(f32[2,512,384]{2,1,0:T(8,128)S(1)} %copy-done.3, bf16[1024,384]{1,0:T(8,128)(2,1)S(1)} %get-tuple-element.49, bf16[1024,3072]{1,0:T(8,128)(2,1)} %constant_dynamic-update-slice_fusion, bf16[1536,384]{1,0:T(8,128)(2,1)S(1)} %copy-done.4, bf16[1536,384]{1,0:T(8,128)(2,1)S(1)} %copy-done.5, pred[]{:T(512)S(6)} %eq.15, ...), kind=kOutput, calls=%fused_computation.27 | convolution fusion | flops 2429681664 | bytes 11014149 | tf_op jit(solution)/shard_map/dot_general | solution.py:114
  194.2 58.8 %all-reduce = f32[32]{0:T(128)S(1)} all-reduce(f32[32]{0:T(128)S(1)} %dynamic-update-slice), channel_id=1, replica_groups=mesh['yh'=2,'z'=8,'xh'=2,'xl'=2,'yl'=2,'c'=2] {'yh','xh','xl','yl','c'}, use_global_device_ids=true, to_apply=%add | all-reduce | flops 32 | bytes 256
  254.4 5.1 %fusion.23 = bf16[8,96,384]{2,1,0:T(8,128)(2,1)} fusion(bf16[8,96,384]{2,1,0:T(8,128)(2,1)S(1)} %collective-permute-done.18, bf16[8,96,384]{2,1,0:T(8,128)(2,1)} %collective-permute-done.17, bf16[8,96,384]{2,1,0:T(8,128)(2,1)} %collective-permute-done.16, f32[]{:T(128)} %bitcast.34, f32[]{:T(128)} %bitcast.32, f32[]{:T(128)} %bitcast.30, ...), kind=kLoop, calls=%fused_computation.38 | loop fusion | flops 3538944 | bytes 2949144 | tf_op jit(solution)/shard_map/convert_element_type | solution.py:132
  259.5 14.5 %all-to-all-start = ((bf16[16,48,384]{2,1,0:T(8,128)(2,1)}), bf16[16,48,384]{2,1,0:T(8,128)(2,1)S(1)}, u32[]{:S(2)}, u32[]{:S(2)}) async-start(bf16[16,48,384]{2,1,0:T(8,128)(2,1)} %bitcast.36), calls=%async_computation | async-start | bytes 1179648 | tf_op jit(solution)/shard_map/all_to_all | solution.py:134
  274.0 1.5 collective-permute-start.19
  275.5 10.6 %collective-permute-done.19 = f32[]{:T(128)} collective-permute-done((f32[]{:T(128)}, f32[]{:T(128)}, u32[]{:S(2)}, u32[]{:S(2)}) %collective-permute-start.19) | collective-permute-done | bytes 36 | tf_op jit(solution)/shard_map/ppermute | solution.py:120
  287.3 2.2 collective-permute-start.20
  289.5 2.5 collective-permute-done.20
  292.6 5.8 %collective-permute-start.21 = (f32[]{:T(128)}, f32[]{:T(128)}, u32[]{:S(2)}, u32[]{:S(2)}) collective-permute-start(f32[]{:T(128)} %add.285), channel_id=1, source_target_pairs={{0,64},{16,80},{32,96},{48,112},{64,0},{80,16},{96,32},{112,48},{1... | collective-permute-start | bytes 20 | tf_op jit(solution)/shard_map/ppermute | solution.py:120
  298.4 1.8 collective-permute-done.21
  (98 shorter events, 32.2 us)
Async XLA Ops:
  7.2 157.2 %all-gather.2.cloned.1.call-start = ((), (), s32[]{:S(2)}) async-start(), calls=%async_computation.1 | async-start | bytes 2433024 | tf_op jit(solution)/shard_map/all_gather | solution.py:62
  13.1 65.1 %collective-permute-start.4 = (bf16[128,3072]{1,0:T(8,128)(2,1)}, bf16[128,3072]{1,0:T(8,128)(2,1)S(1)}, u32[]{:S(2)}, u32[]{:S(2)}) collective-permute-start(bf16[128,3072]{1,0:T(8,128)(2,1)} %get-tuple-element.8), channel_id=1, source_target_pairs={{0,2},{2,0},{1,3},{3,1},{4,6},{6,4},{5,7},{7,5},{8,10},{10,8},{9,1... | collective-permute-start | bytes 2359304 | tf_op jit(solution)/shard_map/ppermute | solution.py:33
  14.7 64.0 %collective-permute-start.7 = (bf16[128,3072]{1,0:T(8,128)(2,1)}, bf16[128,3072]{1,0:T(8,128)(2,1)S(1)}, u32[]{:S(2)}, u32[]{:S(2)}) collective-permute-start(bf16[128,3072]{1,0:T(8,128)(2,1)} %get-tuple-element.8), channel_id=1, source_target_pairs={{0,4},{4,0},{1,5},{5,1},{2,6},{6,2},{3,7},{7,3},{8,12},{12,8},{9,1... | collective-permute-start | bytes 2359304 | tf_op jit(solution)/shard_map/ppermute | solution.py:33
  15.4 5.1 %copy-start.6 = (f32[48,768]{1,0:T(8,128)S(1)}, f32[48,768]{1,0:T(8,128)}, u32[]{:S(2)}) copy-start(f32[48,768]{1,0:T(8,128)} %param.15) | copy-start | bytes 442372
  15.4 8.8 %copy-start.11 = (s32[32]{0:T(128)S(1)}, s32[32]{0:T(128)}, u32[]{:S(2)}) copy-start(s32[32]{0:T(128)} %param.12) | copy-start | bytes 388
  16.9 34.7 %collective-permute-start.2 = (bf16[2,128,384]{2,1,0:T(8,128)(2,1)}, bf16[2,128,384]{2,1,0:T(8,128)(2,1)}, u32[]{:S(2)}, u32[]{:S(2)}) collective-permute-start(bf16[2,128,384]{2,1,0:T(8,128)(2,1)} %pad_maximum_fusion.3), channel_id=1, source_target_pairs={{0,6},{2,4},{4,2},{6,0},{1,7},{3,5},{5,3},{7,1},{8,14},{10,12},{12... | collective-permute-start | bytes 589832 | tf_op jit(solution)/shard_map/ppermute | solution.py:33
  19.2 26.2 %collective-permute-start = (bf16[4,128,384]{2,1,0:T(8,128)(2,1)}, bf16[4,128,384]{2,1,0:T(8,128)(2,1)}, u32[]{:S(2)}, u32[]{:S(2)}) collective-permute-start(bf16[4,128,384]{2,1,0:T(8,128)(2,1)} %pad_maximum_fusion.1), channel_id=1, source_target_pairs={{0,2},{2,0},{1,3},{3,1},{4,6},{6,4},{5,7},{7,5},{8,10},{10,8},{9,1... | collective-permute-start | bytes 1179656 | tf_op jit(solution)/shard_map/ppermute | solution.py:33
  22.6 16.5 %collective-permute-start.12 = (bf16[48,384]{1,0:T(8,128)(2,1)}, bf16[48,384]{1,0:T(8,128)(2,1)}, u32[]{:S(2)}, u32[]{:S(2)}) collective-permute-start(bf16[48,384]{1,0:T(8,128)(2,1)} %get-tuple-element.41), channel_id=1, source_target_pairs={{0,4},{4,0},{1,5},{5,1},{2,6},{6,2},{3,7},{7,3},{8,12},{12,8},{9,1... | collective-permute-start | bytes 110600 | tf_op jit(solution)/shard_map/ppermute | solution.py:33
  39.1 9.5 %collective-permute-start.1 = (bf16[2,128,384]{2,1,0:T(8,128)(2,1)S(1)}, bf16[2,128,384]{2,1,0:T(8,128)(2,1)}, u32[]{:S(2)}, u32[]{:S(2)}) collective-permute-start(bf16[2,128,384]{2,1,0:T(8,128)(2,1)S(1)} %pad_maximum_fusion.2), channel_id=1, source_target_pairs={{0,4},{4,0},{1,5},{5,1},{2,6},{6,2},{3,7},{7,3},{8,12},{12,8},{9,1... | collective-permute-start | bytes 589832 | tf_op jit(solution)/shard_map/ppermute | solution.py:33
  45.4 16.6 %collective-permute-start.15 = (bf16[768,384]{1,0:T(8,128)(2,1)S(1)}, bf16[768,384]{1,0:T(8,128)(2,1)S(1)}, u32[]{:S(2)}, u32[]{:S(2)}) collective-permute-start(bf16[768,384]{1,0:T(8,128)(2,1)S(1)} %get-tuple-element.11), channel_id=1, source_target_pairs={{0,131},{1,130},{2,129},{3,128},{128,3},{129,2},{130,1},{131,0},{4... | collective-permute-start | bytes 1769480 | tf_op jit(solution)/shard_map/ppermute | solution.py:33
  48.6 26.8 %collective-permute-start.14 = (bf16[768,384]{1,0:T(8,128)(2,1)}, bf16[768,384]{1,0:T(8,128)(2,1)S(1)}, u32[]{:S(2)}, u32[]{:S(2)}) collective-permute-start(bf16[768,384]{1,0:T(8,128)(2,1)} %get-tuple-element.12), channel_id=1, source_target_pairs={{0,130},{2,128},{128,2},{130,0},{1,131},{3,129},{129,3},{131,1},{4... | collective-permute-start | bytes 1769480 | tf_op jit(solution)/shard_map/ppermute | solution.py:33
  51.6 25.2 %collective-permute-start.13 = (bf16[768,384]{1,0:T(8,128)(2,1)}, bf16[768,384]{1,0:T(8,128)(2,1)S(1)}, u32[]{:S(2)}, u32[]{:S(2)}) collective-permute-start(bf16[768,384]{1,0:T(8,128)(2,1)} %get-tuple-element.10), channel_id=1, source_target_pairs={{0,1},{1,0},{2,3},{3,2},{4,5},{5,4},{6,7},{7,6},{8,9},{9,8},{10,11... | collective-permute-start | bytes 1769480 | tf_op jit(solution)/shard_map/ppermute | solution.py:33
  62.0 18.4 %collective-permute-start.5 = (bf16[128,3072]{1,0:T(8,128)(2,1)}, bf16[128,3072]{1,0:T(8,128)(2,1)S(1)}, u32[]{:S(2)}, u32[]{:S(2)}) collective-permute-start(bf16[128,3072]{1,0:T(8,128)(2,1)} %get-tuple-element.8), channel_id=1, source_target_pairs={{0,1},{1,0},{2,3},{3,2},{4,5},{5,4},{6,7},{7,6},{8,9},{9,8},{10,11... | collective-permute-start | bytes 2359304 | tf_op jit(solution)/shard_map/ppermute | solution.py:33
  75.4 6.5 %collective-permute-start.3 = (bf16[6,128,384]{2,1,0:T(8,128)(2,1)}, bf16[6,128,384]{2,1,0:T(8,128)(2,1)S(1)}, u32[]{:S(2)}, u32[]{:S(2)}) collective-permute-start(bf16[6,128,384]{2,1,0:T(8,128)(2,1)} %get-tuple-element.37), channel_id=1, source_target_pairs={{0,1},{1,0},{2,3},{3,2},{4,5},{5,4},{6,7},{7,6},{8,9},{9,8},{10,11... | collective-permute-start | bytes 1769480 | tf_op jit(solution)/shard_map/ppermute | solution.py:33
  78.3 11.6 %collective-permute-start.8 = (bf16[64,3072]{1,0:T(8,128)(2,1)S(1)}, bf16[64,3072]{1,0:T(8,128)(2,1)S(1)}, u32[]{:S(2)}, u32[]{:S(2)}) collective-permute-start(bf16[64,3072]{1,0:T(8,128)(2,1)S(1)} %slice.81), channel_id=1, source_target_pairs={{0,4},{4,0},{1,5},{5,1},{2,6},{6,2},{3,7},{7,3},{8,12},{12,8},{9,1... | collective-permute-start | bytes 1179656 | tf_op jit(solution)/shard_map/ppermute | solution.py:33
  78.8 11.3 %collective-permute-start.9 = (bf16[64,3072]{1,0:T(8,128)(2,1)S(1)}, bf16[64,3072]{1,0:T(8,128)(2,1)S(1)}, u32[]{:S(2)}, u32[]{:S(2)}) collective-permute-start(bf16[64,3072]{1,0:T(8,128)(2,1)S(1)} %slice.82), channel_id=1, source_target_pairs={{0,2},{2,0},{1,3},{3,1},{4,6},{6,4},{5,7},{7,5},{8,10},{10,8},{9,1... | collective-permute-start | bytes 1179656 | tf_op jit(solution)/shard_map/ppermute | solution.py:33
  79.5 10.8 %collective-permute-start.6 = (bf16[128,3072]{1,0:T(8,128)(2,1)S(1)}, bf16[128,3072]{1,0:T(8,128)(2,1)S(1)}, u32[]{:S(2)}, u32[]{:S(2)}) collective-permute-start(bf16[128,3072]{1,0:T(8,128)(2,1)S(1)} %collective-permute-done.4), channel_id=1, source_target_pairs={{0,1},{1,0},{2,3},{3,2},{4,5},{5,4},{6,7},{7,6},{8,9},{9,8},{10,11... | collective-permute-start | bytes 2359304 | tf_op jit(solution)/shard_map/ppermute | solution.py:33
  80.4 13.3 %collective-permute-start.10 = (bf16[128,3072]{1,0:T(8,128)(2,1)S(1)}, bf16[128,3072]{1,0:T(8,128)(2,1)S(1)}, u32[]{:S(2)}, u32[]{:S(2)}) collective-permute-start(bf16[128,3072]{1,0:T(8,128)(2,1)S(1)} %collective-permute-done.7), channel_id=1, source_target_pairs={{0,1},{1,0},{2,3},{3,2},{4,5},{5,4},{6,7},{7,6},{8,9},{9,8},{10,11... | collective-permute-start | bytes 2359304 | tf_op jit(solution)/shard_map/ppermute | solution.py:33
  82.5 82.0 %copy-start.2 = (f32[2,512,384]{2,1,0:T(8,128)}, f32[2,512,384]{2,1,0:T(8,128)S(1)}, u32[]{:S(2)}) copy-start(f32[2,512,384]{2,1,0:T(8,128)S(1)} %fusion.8) | copy-start | bytes 4718596
  90.2 4.5 %collective-permute-start.11 = (bf16[128,3072]{1,0:T(8,128)(2,1)S(1)}, bf16[128,3072]{1,0:T(8,128)(2,1)S(1)}, u32[]{:S(2)}, u32[]{:S(2)}) collective-permute-start(bf16[128,3072]{1,0:T(8,128)(2,1)S(1)} %pad_maximum_fusion), channel_id=1, source_target_pairs={{0,1},{1,0},{2,3},{3,2},{4,5},{5,4},{6,7},{7,6},{8,9},{9,8},{10,11... | collective-permute-start | bytes 2359304 | tf_op jit(solution)/shard_map/ppermute | solution.py:33
  171.3 14.3 %copy-start.5 = (bf16[1536,384]{1,0:T(8,128)(2,1)S(1)}, bf16[1536,384]{1,0:T(8,128)(2,1)}, u32[]{:S(2)}) copy-start(bf16[1536,384]{1,0:T(8,128)(2,1)} %maximum_select_fusion.4) | copy-start | bytes 3538948
  177.7 7.9 %copy-start.3 = (f32[2,512,384]{2,1,0:T(8,128)S(1)}, f32[2,512,384]{2,1,0:T(8,128)}, u32[]{:S(2)}) copy-start(f32[2,512,384]{2,1,0:T(8,128)} %copy-done.2) | copy-start | bytes 4718596
  177.7 7.9 %copy-start.4 = (bf16[1536,384]{1,0:T(8,128)(2,1)S(1)}, bf16[1536,384]{1,0:T(8,128)(2,1)}, u32[]{:S(2)}) copy-start(bf16[1536,384]{1,0:T(8,128)(2,1)} %maximum_select_fusion.5) | copy-start | bytes 3538948
  179.1 75.3 %collective-permute-start.18 = (bf16[8,96,384]{2,1,0:T(8,128)(2,1)}, bf16[8,96,384]{2,1,0:T(8,128)(2,1)S(1)}, u32[]{:S(2)}, u32[]{:S(2)}) collective-permute-start(bf16[8,96,384]{2,1,0:T(8,128)(2,1)} %get-tuple-element.14), channel_id=1, source_target_pairs={{0,136},{8,128},{128,8},{136,0},{1,137},{9,129},{129,9},{137,1},{2... | collective-permute-start | bytes 1769480 | tf_op jit(solution)/shard_map/ppermute | solution.py:33
  182.1 72.3 %collective-permute-start.17 = (bf16[8,96,384]{2,1,0:T(8,128)(2,1)}, bf16[8,96,384]{2,1,0:T(8,128)(2,1)}, u32[]{:S(2)}, u32[]{:S(2)}) collective-permute-start(bf16[8,96,384]{2,1,0:T(8,128)(2,1)} %get-tuple-element.15), channel_id=1, source_target_pairs={{0,128},{128,0},{1,129},{129,1},{2,130},{130,2},{3,131},{131,3},{4... | collective-permute-start | bytes 1769480 | tf_op jit(solution)/shard_map/ppermute | solution.py:33
  184.1 70.2 %collective-permute-start.16 = (bf16[8,96,384]{2,1,0:T(8,128)(2,1)}, bf16[8,96,384]{2,1,0:T(8,128)(2,1)}, u32[]{:S(2)}, u32[]{:S(2)}) collective-permute-start(bf16[8,96,384]{2,1,0:T(8,128)(2,1)} %get-tuple-element.13), channel_id=1, source_target_pairs={{0,8},{8,0},{1,9},{9,1},{2,10},{10,2},{3,11},{11,3},{4,12},{12,4},... | collective-permute-start | bytes 1769480 | tf_op jit(solution)/shard_map/ppermute | solution.py:33
  259.5 41.5 %copy-start.7 = (f32[48,768]{1,0:T(8,128)S(1)}, f32[48,768]{1,0:T(8,128)}, u32[]{:S(2)}) copy-start(f32[48,768]{1,0:T(8,128)} %param.16) | copy-start | bytes 442372
  259.5 41.5 %copy-start.8 = (f32[48,768]{1,0:T(8,128)S(1)}, f32[48,768]{1,0:T(8,128)}, u32[]{:S(2)}) copy-start(f32[48,768]{1,0:T(8,128)} %param.17) | copy-start | bytes 442372
  259.5 41.4 %all-to-all-start = ((bf16[16,48,384]{2,1,0:T(8,128)(2,1)}), bf16[16,48,384]{2,1,0:T(8,128)(2,1)S(1)}, u32[]{:S(2)}, u32[]{:S(2)}) async-start(bf16[16,48,384]{2,1,0:T(8,128)(2,1)} %bitcast.36), calls=%async_computation | async-start | bytes 1179648 | tf_op jit(solution)/shard_map/all_to_all | solution.py:134
  274.0 12.0 %collective-permute-start.19 = (f32[]{:T(128)}, f32[]{:T(128)}, u32[]{:S(2)}, u32[]{:S(2)}) collective-permute-start(f32[]{:T(128)} %get-tuple-element.42), channel_id=1, source_target_pairs={{0,16},{16,0},{32,48},{48,32},{64,80},{80,64},{96,112},{112,96},{1... | collective-permute-start | bytes 20 | tf_op jit(solution)/shard_map/ppermute | solution.py:120
  287.3 4.6 %collective-permute-start.20 = (f32[]{:T(128)}, f32[]{:T(128)}, u32[]{:S(2)}, u32[]{:S(2)}) collective-permute-start(f32[]{:T(128)} %add.284), channel_id=1, source_target_pairs={{0,32},{16,48},{32,0},{48,16},{64,96},{80,112},{96,64},{112,80},{1... | collective-permute-start | bytes 20 | tf_op jit(solution)/shard_map/ppermute | solution.py:120
  292.6 7.6 %collective-permute-start.21 = (f32[]{:T(128)}, f32[]{:T(128)}, u32[]{:S(2)}, u32[]{:S(2)}) collective-permute-start(f32[]{:T(128)} %add.285), channel_id=1, source_target_pairs={{0,64},{16,80},{32,96},{48,112},{64,0},{80,16},{96,32},{112,48},{1... | collective-permute-start | bytes 20 | tf_op jit(solution)/shard_map/ppermute | solution.py:120
  (5 other events, 15.5 us)
Sparse Core Ops, SparseCore 0:
  41.2 123.1 all-gather.1

commit v2 on v1

v2 whole, which is shorter than its diff:
```python
import jax
import jax.numpy as jnp
import numpy as np
from jax import lax
from jax.experimental import pallas as pl
from jax.experimental.pallas import tpu as pltpu
from jax.sharding import Mesh
from jax.sharding import PartitionSpec as P

STEPS = 1000
ADAM_STEP = 100
BETA = 5000.0
AXES = ("yh", "z", "xh", "xl", "yl", "c")
SIZES = (2, 8, 2, 2, 2, 2)
bf16 = jnp.bfloat16
f32 = jnp.float32


def normalize(noisy, gain):
    mean_sq = jnp.mean(noisy * noisy, axis=1, keepdims=True)
    return jax.nn.gelu(noisy * lax.rsqrt(mean_sq + 1e-06) * gain, approximate=True).astype(bf16)


def adam_update(master, first, second, gradient):
    new_first = 0.9 * first + 0.1 * gradient
    new_second = 0.999 * second + 0.001 * gradient * gradient
    first_hat = new_first / (1.0 - 0.9**ADAM_STEP)
    second_hat = new_second / (1.0 - 0.999**ADAM_STEP)
    new_master = master - 0.001 * (first_hat / (jnp.sqrt(second_hat) + 1e-08) + 0.01 * master)
    return (new_master, new_first, new_second)


def flip(x, *axes):
    last = 2 ** len(axes) - 1
    return lax.ppermute(x, axes, [(i, last - i) for i in range(last + 1)])


def shift(x, step):
    return lax.ppermute(x, "z", [(i, (i + step) % SIZES[1]) for i in range(SIZES[1])])


def after(x, *others):
    return lax.optimization_barrier((x,) + others)[0]


def ordered(index, own, other):
    return jnp.where(
        index == 0, jnp.concatenate([own, other]), jnp.concatenate([other, own])
    )


def pack_kernel(half, at, timestep, latents, noise, gain, feats, send_y, send_x, send_c):
    time = (timestep[at[0]].astype(f32) + 0.5) / STEPS
    clean, drawn = latents[...].astype(f32), noise[...].astype(f32)
    value = normalize((1.0 - time) * clean + time * drawn, gain[...])
    width = value.shape[1]
    low, high = value[:, : width // 2], value[:, width // 2 :]
    value = jnp.where(at[1] == 0, value, jnp.concatenate([high, low], 1))

    def fill(out, places, after_feats):
        col = 0
        for array, place in places:
            start = pl.multiple_of(at[place] * half, 128)
            out[:, col : col + half] = array[:, pl.ds(start, half)]
            col += half
        out[:, col : col + width] = value
        col += width
        for array, place in after_feats:
            start = pl.multiple_of(at[place] * half, 128)
            out[:, col : col + half] = array[:, pl.ds(start, half)]
            col += half

    diagonal = [(latents, 8), (latents, 7)]
    feats[...] = value
    fill(send_y, [(latents, 3), (noise, 3), (latents, 4), (noise, 4)], diagonal)
    fill(send_x, [(latents, 5), (latents, 6)], diagonal)
    fill(send_c, [(latents, 2), (noise, 2)], [])


def pack(at, timestep, latents, noise, gain, half):
    tok, width = latents.shape
    rows = tok // 4
    widths = (width, width + 6 * half, width + 4 * half, width + 2 * half)
    small = pl.BlockSpec(memory_space=pltpu.SMEM)
    return pl.pallas_call(
        lambda *refs: pack_kernel(half, *refs),
        grid=(tok // rows,),
        in_specs=[
            small,
            small,
            pl.BlockSpec((rows, width), lambda i: (i, 0)),
            pl.BlockSpec((rows, width), lambda i: (i, 0)),
            pl.BlockSpec((1, width), lambda i: (0, 0)),
        ],
        out_specs=[pl.BlockSpec((rows, w), lambda i: (i, 0)) for w in widths],
        out_shape=[jax.ShapeDtypeStruct((tok, w), bf16) for w in widths],
        compiler_params=pltpu.CompilerParams(vmem_limit_bytes=16 * 2**20),
        cost_estimate=pl.CostEstimate(
            flops=20 * tok * width, bytes_accessed=15 * tok * width, transcendentals=tok * width
        ),
        name="pack",
    )(at, timestep, latents, noise, gain[None])


def project_kernel(
    half, at, timestep, winner, latents, noise, feats, got_y, got_c, got_yc, got_x, diag_0, diag_1,
    got_xc, diag_c0, diag_c1, policy, reference, ref_y, ref_c, gap, near, near_x, far, far_x,
    rows_ref, both, clean, drawn, grad, sems,
):
    tok, width = feats.shape
    h = tok // 2
    pair, yh, yl, c, xh, xl, own = (at[i] for i in range(7))
    time = (timestep[pair].astype(f32) + 0.5) / STEPS
    sign = jnp.where(winner[pair] == xl, 1.0, -1.0).astype(f32)
    mine = pl.ds(pl.multiple_of(own * half, 128), half)
    count = [0]

    def start(source, target):
        copy = pltpu.make_async_copy(source, target, sems.at[count[0]])
        count[0] += 1
        copy.start()
        return copy

    def lanes(first, size=half):
        return pl.ds(first * half, size)

    def rows_of(k):
        return pl.ds(k * tok, tok)

    n_z, depth = policy.shape[0], policy.shape[2]
    weight_copies = [
        start(policy.at[z, y], both.at[pl.ds((y * n_z + z) * depth, depth), lanes(0)])
        for z in range(n_z)
        for y in range(2)
    ]
    block = reference.shape[0]
    for dy, dc, source in (
        (0, 0, reference.at[:, mine]),
        (0, 1, ref_c.at[:, lanes(0)]),
        (1, 0, ref_y.at[:, lanes(0)]),
        (1, 1, ref_c.at[:, lanes(1)]),
    ):
        place = ((yl ^ dy ^ yh) * 2 + (c ^ dc)) * block
        target = both.at[pl.ds(pl.multiple_of(place, block), block), lanes(1)]
        weight_copies.append(start(source, target))

    def piece(k, source, feats_at, clean_at, drawn_at):
        copies = [
            start(source.at[:, lanes(feats_at, width)], rows_ref.at[rows_of(k)]),
            start(source.at[:, lanes(clean_at)], clean.at[rows_of(k)]),
        ]
        if drawn_at is not None:
            copies.append(start(source.at[:, lanes(drawn_at)], drawn.at[rows_of(k)]))
        return copies

    def halves(k, source):
        copies = []
        for i in range(2):
            part, rows = source[i], pl.ds(k * tok + i * h, h)
            copies.append(start(part.at[:, lanes(0, width)], rows_ref.at[rows]))
            copies.append(start(part.at[:, lanes(9 if k == 5 else 8)], clean.at[rows]))
        return copies

    chunks = [
        [
            start(feats, rows_ref.at[rows_of(0)]),
            start(latents.at[:, mine], clean.at[rows_of(0)]),
            start(noise.at[:, mine], drawn.at[rows_of(0)]),
        ]
        + piece(1, got_y, 4, 0, 1),
        piece(2, got_c, 2, 0, 1) + piece(3, got_yc, 4, 2, 3),
        piece(4, got_x, 2, 0, None) + halves(5, (diag_0, diag_1)),
        piece(6, got_xc, 2, 1, None) + halves(7, (diag_c0, diag_c1)),
    ]
    for copy in weight_copies:
        copy.wait()
    total = jnp.zeros((1, half), f32)
    for i, copies in enumerate(chunks):
        for copy in copies:
            copy.wait()
        rows = pl.ds(i * 2 * tok, 2 * tok)
        out = jnp.dot(rows_ref[rows, :], both[...], preferred_element_type=f32)
        start_rows = clean[rows, :].astype(f32)
        noise_rows = drawn[pl.ds((i % 2) * 2 * tok, 2 * tok), :].astype(f32)
        base = ((1.0 - time) * start_rows + time * noise_rows) - (noise_rows - start_rows)
        policy_diff = base + out[:, :half].astype(bf16).astype(f32)
        ref_diff = base + out[:, half:]
        signed = sign if i < 2 else -sign
        grad[rows, :] = (signed * policy_diff).astype(bf16)
        excess = policy_diff * policy_diff - ref_diff * ref_diff
        total = total + signed * jnp.sum(excess, axis=0, keepdims=True)
    gap[...] = jnp.broadcast_to(jnp.sum(total, axis=1, keepdims=True), gap.shape)

    per = depth // 2
    for y, same, other in ((1, far, far_x), (0, near, near_x)):
        for z in range(0, n_z, 2):
            part = lax.dot_general(
                rows_ref[:, pl.ds((y * n_z + z) * depth, 2 * depth)],
                grad[...],
                (((0,), (0,)), ((), ())),
                preferred_element_type=f32,
            ).astype(bf16)
            for k in range(2):
                low = part[2 * k * per : (2 * k + 1) * per]
                high = part[(2 * k + 1) * per : (2 * k + 2) * per]
                rows = pl.ds((z + k) * per, per)
                same[rows, :] = jnp.where(xh == 0, low, high)
                other[rows, :] = jnp.where(xh == 0, high, low)
    tail = pl.ds(n_z * per, 16)
    for out in (near, near_x, far, far_x):
        out[tail, :] = jnp.zeros((16, half), bf16)


def project(at, timestep, winner, half, *arrays):
    tok, width = arrays[2].shape
    policy = arrays[12]
    out_rows = policy.shape[0] * policy.shape[2] // 2 + 16
    small = pl.BlockSpec(memory_space=pltpu.SMEM)
    block = jax.ShapeDtypeStruct((out_rows, half), bf16)
    return pl.pallas_call(
        lambda *refs: project_kernel(half, *refs),
        in_specs=[small] * 3 + [pl.BlockSpec(memory_space=pl.ANY)] * len(arrays),
        out_specs=[pl.BlockSpec(memory_space=pltpu.VMEM)] * 5,
        out_shape=[jax.ShapeDtypeStruct((8, 128), f32)] + [block] * 4,
        scratch_shapes=[
            pltpu.VMEM((8 * tok, width), bf16),
            pltpu.VMEM((width, 2 * half), bf16),
            pltpu.VMEM((8 * tok, half), bf16),
            pltpu.VMEM((4 * tok, half), bf16),
            pltpu.VMEM((8 * tok, half), bf16),
            pltpu.SemaphoreType.DMA((48,)),
        ],
        compiler_params=pltpu.CompilerParams(vmem_limit_bytes=40 * 2**20),
        cost_estimate=pl.CostEstimate(
            flops=6 * 8 * tok * width * half, bytes_accessed=16 * 2**20, transcendentals=0
        ),
        name="project",
    )(at, timestep, winner, *arrays)


def body(
    latents, noise, timestep, winner, norm_gain, reference_weight, policy_master, moment_first, moment_second
):
    tok, width = latents.shape
    yh, z, xh, xl, yl, c = (lax.axis_index(a) for a in AXES)
    half = policy_master.shape[1] // 2
    pair = (yh * SIZES[1] + z) * SIZES[2] + xh
    count_pairs = timestep.shape[0]
    scale = float(4 * tok * width)
    def columns(array, dx, dy, dc):
        block = ((yl ^ dy) * 2 + (c ^ dc)) * 2 + (xl ^ dx)
        return lax.dynamic_slice_in_dim(array, block * half, half, 1)

    policy_bf = policy_master.astype(bf16)
    own_w = lax.dynamic_slice_in_dim(policy_bf, xl * half, half, 1)
    other_w = flip(lax.dynamic_slice_in_dim(policy_bf, (1 - xl) * half, half, 1), "xl")
    own_w = ordered(xl, own_w, other_w)
    same_z = jnp.stack(
        [
            ordered(xh, own_w[None], flip(own_w, "xh")[None]),
            ordered(xh, flip(own_w, "yh")[None], flip(own_w, "yh", "xh")[None]),
        ]
    )[:, None]

    blocks = [
        ((yl ^ dy) * 2 + (c ^ dc)) * 2 + (xl ^ dx)
        for dx, dy in ((0, 0), (0, 1), (1, 0), (1, 1))
        for dc in (0, 1)
    ]
    at = jnp.stack([pair, yh] + blocks[1:])
    feats, send_y, send_x, send_c = pack(at, timestep, latents, noise, norm_gain, half)
    send_y, send_x, send_c, weight_in, _ = lax.optimization_barrier(
        (send_y, send_x, send_c, reference_weight, same_z)
    )
    got_y, got_x, got_c = flip(send_y, "yl"), flip(send_x, "xl"), flip(send_c, "c")

    ref_y = flip(
        jnp.concatenate([columns(weight_in, 0, 1, 0), columns(weight_in, 0, 1, 1)], 1), "yh", "yl"
    )
    ref_c = flip(jnp.concatenate([columns(weight_in, 0, 0, 1), ref_y[:, half:]], 1), "c")
    n_z = SIZES[1]
    per_z = lax.all_gather(same_z.reshape(-1, half), "z").reshape(n_z, 2, -1, half)

    h = tok // 2
    diag = [flip(got_y[:h, 4 * half :], "xl"), flip(got_x[h:, 2 * half :], "yl")]
    diag_c = [flip(part, "c") for part in diag]
    got_yc, got_xc = flip(got_y, "c"), flip(got_x, "c")

    places = jnp.stack([pair, yh, yl, c, xh, xl, blocks[0]])
    gap, near, near_x, far, far_x = project(
        places, timestep, winner, half, latents, noise, feats, got_y, got_c, got_yc, got_x,
        *diag, got_xc, *diag_c, per_z, reference_weight, ref_y, ref_c,
    )

    gap = gap[:1, :1]
    gap = gap + flip(gap, "c")
    gap = flip(gap, "xl") + flip(gap, "yl") + (flip(gap, "xl", "yl") + gap)
    margin = -0.5 * BETA * (gap / scale)
    first = lax.reduce_precision(margin, 8, 7)
    second = lax.reduce_precision(margin - first, 8, 7)
    terms = jnp.concatenate([first, second, (margin - first) - second]).astype(bf16)
    terms = jnp.broadcast_to(jnp.concatenate([terms, jnp.zeros((13, 1), bf16)]), (16, half))
    size = near.shape[0] - 16

    def with_margin(block):
        return lax.dynamic_update_slice(block, terms, (size, 0))

    got = [
        near,
        flip(with_margin(near_x), "xh"),
        flip(with_margin(far), "yh"),
        flip(with_margin(far_x), "yh", "xh"),
    ]

    def margin_of(block):
        first, second, third = (block[size + i : size + i + 1, :1].astype(f32) for i in range(3))
        return (first + second) + third

    margins = [margin] + [margin_of(g) for g in got[1:]]
    weights = [
        jax.nn.sigmoid(-m) * BETA / (2.0 * count_pairs) * (2.0 / scale) for m in margins
    ]
    losses = [jax.nn.softplus(-m) for m in margins]
    loss = ((losses[0] + losses[1]) + (losses[2] + losses[3])).reshape(())
    for step in (1, 2, 4):
        loss = loss + lax.ppermute(loss, "z", [(i, i ^ step) for i in range(n_z)])
    loss = loss / count_pairs
    got = [g[:size] for g in got]

    summed = sum(w * g.astype(f32) for w, g in zip(weights, got)).astype(bf16)
    rows = policy_master.shape[0]
    blocks = lax.all_to_all(
        summed.reshape(-1, rows, half), ("z", "xl"), split_axis=0, concat_axis=0, tiled=True
    )
    blocks = blocks.reshape(SIZES[1], 2, rows, half).astype(f32).sum(axis=0)
    gradient = jnp.concatenate([blocks[0], blocks[1]], axis=1)
    return adam_update(policy_master, moment_first, moment_second, gradient) + (loss,)


def solution(mesh):
    fine = Mesh(mesh.devices.reshape(SIZES), AXES)
    fsdp, tp = AXES[:4], AXES[4:]
    return jax.shard_map(
        body,
        mesh=fine,
        in_specs=(P(AXES, None), P(AXES, None), P(), P(), P(), P(tp, None))
        + (P(fsdp, tp),) * 3,
        out_specs=(P(fsdp, tp), P(fsdp, tp), P(fsdp, tp), P()),
        check_vma=False,
    )
```

time: 311 us -> 191 us (0.61)
  blocking collectives: 58.8 us -> 0 us
  waiting for transfers between devices: 125 us -> 72.4 us
  matrix products: 20.4 us -> 0 us
  Pallas kernels: 0 us -> 17.5 us
  local copies, waits for them, and re-layouts: 25.2 us -> 8.36 us
  starting transfers between devices: 42.9 us -> 56.1 us
  other arithmetic: 18.5 us -> 5.36 us
  between operations: 19.3 us -> 30.3 us
    all_gather x1, waiting for transfers between devices: 68.8 us -> 0.01 us  [body(): lax.all_gather(same_z.reshape(-1, half), 'z').reshape(n_z, 2, -1, half)]
    unnamed x1 -> x0, blocking collectives: 58.8 us -> none
    ppermute x19 -> x22, waiting for transfers between devices: 41 us -> 64.6 us  [flip(): return lax.ppermute(x, axes, [(i, last - i) for i in range(last + 1)])]
    dot_general x3 -> x0, matrix products: 20.4 us -> none  [the longest x1 7.14 us: body(): ref_diff = base + jnp.dot(group_feats, ref_cols, preferred_element_type=f32)]
    pallas_call x0 -> x2, Pallas kernels: none -> 17.5 us  [the longest x1 14 us: project(): pl.pallas_call(lambda *refs: project_kernel(half, *refs), in_specs=[small...]
    ppermute x19 -> x22, starting transfers between devices: 18.9 us -> 31 us  [flip(): return lax.ppermute(x, axes, [(i, last - i) for i in range(last + 1)])]
    unnamed x39 -> x24, local copies, waits for them, and re-layouts: 10.9 us -> 2.18 us
    ppermute x3, waiting for transfers between devices: 14.8 us -> 7.77 us  [body(): loss = loss + lax.ppermute(loss, 'z', [(i, i ^ step) for i in range(n_z)])]
  transfers between devices with their start and end apart: 24 -> 27, of which waited for: 10 -> 15; matrix products, arithmetic and copies ran while one was open for 12% -> 3% of each run, Pallas kernels for 0% -> 2%
where the time goes in v2:
time: 191 us; the launch traced here: 190 us
  waiting for transfers between devices  72.4 us (38%)
  starting transfers between devices  56.1 us (29%)
  between operations  30.3 us (16%)
  Pallas kernels  17.5 us (9%)
  local copies, waits for them, and re-layouts  8.36 us (4%)
  other arithmetic  5.36 us (3%)
    ppermute x22, waiting for transfers between devices, flip(): return lax.ppermute(x, axes, [(i, last - i) for i in range(last + 1)])  64.6 us
    ppermute x22, starting transfers between devices, flip(): return lax.ppermute(x, axes, [(i, last - i) for i in range(last + 1)])  31 us
    ppermute x3, starting transfers between devices, body(): loss = loss + lax.ppermute(loss, 'z', [(i, i ^ step) for i in range(n_z)])  15.1 us
    pallas_call x1, Pallas kernels, project(): pl.pallas_call(lambda *refs: project_kernel(half, *refs), in_specs=[small...  14 us
    all_to_all x1, starting transfers between devices, body(): lax.all_to_all(summed.reshape(-1, rows, half), ('z', 'xl'), split_axis=0,...  10.1 us
    ppermute x3, waiting for transfers between devices, body(): loss = loss + lax.ppermute(loss, 'z', [(i, i ^ step) for i in range(n_z)])  7.77 us
  transfers between devices with their start and end apart: 27, of which 15 were waited for; matrix products, arithmetic and copies ran while one was open for 3% of the time, Pallas kernels for 2%

profile of v2, /device:TPU:2, one launch (start us, length us, event | category | flops | bytes accessed | tf_op | source)
XLA Modules:
  0.0 190.1 jit_solution(8014819288606404743)
XLA Ops:
  8.3 2.4 %collective-permute-start.9 = (bf16[48,384]{1,0:T(8,128)(2,1)S(1)}, bf16[48,384]{1,0:T(8,128)(2,1)S(1)}, u32[]{:S(2)}, u32[]{:S(2)}) collective-permute-start(bf16[48,384]{1,0:T(8,128)(2,1)S(1)} %get-tuple-element.48), channel_id=1, source_target_pairs={{0,4},{4,0},{1,5},{5,1},{2,6},{6,2},{3,7},{7,3},{8,12},{12,8},{9,1... | collective-permute-start | bytes 110600 | tf_op jit(solution)/shard_map/ppermute | solution.py:35
  10.7 1.9 %collective-permute-done.9 = bf16[48,384]{1,0:T(8,128)(2,1)S(1)} collective-permute-done((bf16[48,384]{1,0:T(8,128)(2,1)S(1)}, bf16[48,384]{1,0:T(8,128)(2,1)S(1)}, u32[]{:S(2)}, u32[]{:S(2)}) %collective-permute-start.9) | collective-permute-done | bytes 36896 | tf_op jit(solution)/shard_map/ppermute | solution.py:35
  12.6 4.6 %collective-permute-start.12 = (bf16[96,384]{1,0:T(8,128)(2,1)S(1)}, bf16[96,384]{1,0:T(8,128)(2,1)S(1)}, u32[]{:S(2)}, u32[]{:S(2)}) collective-permute-start(bf16[96,384]{1,0:T(8,128)(2,1)S(1)} %maximum_select_fusion.3), channel_id=1, source_target_pairs={{0,136},{8,128},{128,8},{136,0},{1,137},{9,129},{129,9},{137,1},{2... | collective-permute-start | bytes 221192 | tf_op jit(solution)/shard_map/ppermute | solution.py:35
  17.6 1.7 collective-permute-start.10
  19.2 1.8 collective-permute-done.12
  21.1 2.0 %collective-permute-done.11 = bf16[96,384]{1,0:T(8,128)(2,1)S(1)} collective-permute-done((bf16[96,384]{1,0:T(8,128)(2,1)S(1)}, bf16[96,384]{1,0:T(8,128)(2,1)S(1)}, u32[]{:S(2)}, u32[]{:S(2)}) %collective-permute-start.11) | collective-permute-done | bytes 73760 | tf_op jit(solution)/shard_map/ppermute | solution.py:35
  24.4 3.5 %pack.1 = (bf16[128,3072]{1,0:T(8,128)(2,1)S(1)}, bf16[128,5376]{1,0:T(8,128)(2,1)}, bf16[128,4608]{1,0:T(8,128)(2,1)}, bf16[128,3840]{1,0:T(8,128)(2,1)S(1)}) custom-call(s32[9]{0:T(128)S(1)} %stack.70.refs_0_, s32[32]{0:T(128)S(1)} %copy-done.3, bf16[128,3072]{1,0:T(8,128)(2,1)S(1)} %copy-done, bf16[128,3072]{1,0:T(8,128)(2,1)S(1)} %copy-done.1, ...), custom_call_target="tpu_custom_call" | custom-call | flops 7864320 | bytes 5898240 | tf_op jit(solution)/shard_map/pack/pallas_call | solution.py:85
  27.8 1.4 collective-permute-start.3
  29.3 1.6 collective-permute-start
  30.8 1.6 constant_dynamic-slice_fusion
  32.6 2.3 %collective-permute-start.13 = (bf16[768,768]{1,0:T(8,128)(2,1)S(1)}, bf16[768,768]{1,0:T(8,128)(2,1)S(1)}, u32[]{:S(2)}, u32[]{:S(2)}) collective-permute-start(bf16[768,768]{1,0:T(8,128)(2,1)S(1)} %pad_maximum_fusion), channel_id=1, source_target_pairs={{0,130},{2,128},{128,2},{130,0},{1,131},{3,129},{129,3},{131,1},{4... | collective-permute-start | bytes 3538952 | tf_op jit(solution)/shard_map/ppermute | solution.py:35
  34.8 24.1 %collective-permute-done.refs_6_ = bf16[128,5376]{1,0:T(8,128)(2,1)} collective-permute-done((bf16[128,5376]{1,0:T(8,128)(2,1)}, bf16[128,5376]{1,0:T(8,128)(2,1)}, u32[]{:S(2)}, u32[]{:S(2)}) %collective-permute-start) | collective-permute-done | bytes 1376288 | tf_op jit(solution)/shard_map/ppermute | solution.py:35
  65.9 9.6 %collective-permute-done.5.refs_11_ = bf16[64,3840]{1,0:T(8,128)(2,1)} collective-permute-done((bf16[64,3840]{1,0:T(8,128)(2,1)S(1)}, bf16[64,3840]{1,0:T(8,128)(2,1)}, u32[]{:S(2)}, u32[]{:S(2)}) %collective-permute-start.5) | collective-permute-done | bytes 491552 | tf_op jit(solution)/shard_map/ppermute | solution.py:35
  75.5 2.8 %collective-permute-done.4.refs_10_ = bf16[64,3840]{1,0:T(8,128)(2,1)} collective-permute-done((bf16[64,3840]{1,0:T(8,128)(2,1)S(1)}, bf16[64,3840]{1,0:T(8,128)(2,1)}, u32[]{:S(2)}, u32[]{:S(2)}) %collective-permute-start.4) | collective-permute-done | bytes 491552 | tf_op jit(solution)/shard_map/ppermute | solution.py:35
  78.4 2.1 %collective-permute-done.7.refs_13_ = bf16[64,3840]{1,0:T(8,128)(2,1)} collective-permute-done((bf16[64,3840]{1,0:T(8,128)(2,1)}, bf16[64,3840]{1,0:T(8,128)(2,1)}, u32[]{:S(2)}, u32[]{:S(2)}) %collective-permute-start.7) | collective-permute-done | bytes 491552 | tf_op jit(solution)/shard_map/ppermute | solution.py:35
  81.7 14.0 %project.1 = (f32[8,128]{1,0:T(8,128)S(1)}, bf16[784,384]{1,0:T(8,128)(2,1)S(1)}, bf16[784,384]{1,0:T(8,128)(2,1)S(1)}, bf16[784,384]{1,0:T(8,128)(2,1)S(1)}, bf16[784,384]{1,0:T(8,128)(2,1)S(1)}) custom-call(s32[7]{0:T(128)S(1)} %stack.62.refs_0_, s32[32]{0:T(128)S(1)} %copy-done.3, s32[32]{0:T(128)S(1)} %copy-done.8, bf16[128,3072]{1,0:T(8,128)(2,1)S(1)} %copy-done, ...), custom_call_target="tpu_custom_call" | custom-call | flops 7247757312 | bytes 16777216 | tf_op jit(solution)/shard_map/project/pallas_call | solution.py:220
  98.9 2.6 %collective-permute-start.18 = (f32[1,1]{1,0:T(1,128)}, f32[1,1]{1,0:T(1,128)}, u32[]{:S(2)}, u32[]{:S(2)}) collective-permute-start(f32[1,1]{1,0:T(1,128)} %add.185), channel_id=1, source_target_pairs={{0,6},{2,4},{4,2},{6,0},{1,7},{3,5},{5,3},{7,1},{8,14},{10,12},{12... | collective-permute-start | bytes 20 | tf_op jit(solution)/shard_map/ppermute | solution.py:35
  101.5 2.6 %collective-permute-start.17 = (f32[1,1]{1,0:T(1,128)}, f32[1,1]{1,0:T(1,128)}, u32[]{:S(2)}, u32[]{:S(2)}) collective-permute-start(f32[1,1]{1,0:T(1,128)} %add.185), channel_id=1, source_target_pairs={{0,2},{2,0},{1,3},{3,1},{4,6},{6,4},{5,7},{7,5},{8,10},{10,8},{9,1... | collective-permute-start | bytes 20 | tf_op jit(solution)/shard_map/ppermute | solution.py:35
  104.1 2.3 %collective-permute-start.16 = (f32[1,1]{1,0:T(1,128)}, f32[1,1]{1,0:T(1,128)}, u32[]{:S(2)}, u32[]{:S(2)}) collective-permute-start(f32[1,1]{1,0:T(1,128)} %add.185), channel_id=1, source_target_pairs={{0,4},{4,0},{1,5},{5,1},{2,6},{6,2},{3,7},{7,3},{8,12},{12,8},{9,1... | collective-permute-start | bytes 20 | tf_op jit(solution)/shard_map/ppermute | solution.py:35
  112.7 1.8 collective-permute-start.19
  114.6 2.3 %collective-permute-start.20 = (bf16[784,384]{1,0:T(8,128)(2,1)S(1)}, bf16[784,384]{1,0:T(8,128)(2,1)S(1)}, u32[]{:S(2)}, u32[]{:S(2)}) collective-permute-start(bf16[784,384]{1,0:T(8,128)(2,1)S(1)} %get-tuple-element.50), channel_id=1, source_target_pairs={{0,128},{128,0},{1,129},{129,1},{2,130},{130,2},{3,131},{131,3},{4... | collective-permute-start | bytes 1806344 | tf_op jit(solution)/shard_map/ppermute | solution.py:35
  116.9 2.4 %collective-permute-start.21 = (bf16[784,384]{1,0:T(8,128)(2,1)S(1)}, bf16[784,384]{1,0:T(8,128)(2,1)S(1)}, u32[]{:S(2)}, u32[]{:S(2)}) collective-permute-start(bf16[784,384]{1,0:T(8,128)(2,1)S(1)} %get-tuple-element.51), channel_id=1, source_target_pairs={{0,136},{8,128},{128,8},{136,0},{1,137},{9,129},{129,9},{137,1},{2... | collective-permute-start | bytes 1806344 | tf_op jit(solution)/shard_map/ppermute | solution.py:35
  119.3 11.4 %collective-permute-done.19 = bf16[784,384]{1,0:T(8,128)(2,1)S(1)} collective-permute-done((bf16[784,384]{1,0:T(8,128)(2,1)S(1)}, bf16[784,384]{1,0:T(8,128)(2,1)S(1)}, u32[]{:S(2)}, u32[]{:S(2)}) %collective-permute-start.19) | collective-permute-done | bytes 602144 | tf_op jit(solution)/shard_map/ppermute | solution.py:35
  133.3 6.4 %collective-permute-done.20 = bf16[784,384]{1,0:T(8,128)(2,1)S(1)} collective-permute-done((bf16[784,384]{1,0:T(8,128)(2,1)S(1)}, bf16[784,384]{1,0:T(8,128)(2,1)S(1)}, u32[]{:S(2)}, u32[]{:S(2)}) %collective-permute-start.20) | collective-permute-done | bytes 602144 | tf_op jit(solution)/shard_map/ppermute | solution.py:35
  144.8 1.3 add_convert_fusion
  146.1 10.1 %all-to-all-start = ((bf16[16,48,384]{2,1,0:T(8,128)(2,1)}), bf16[16,48,384]{2,1,0:T(8,128)(2,1)S(1)}, u32[]{:S(2)}, u32[]{:S(2)}) async-start(bf16[16,48,384]{2,1,0:T(8,128)(2,1)} %bitcast.27), calls=%async_computation | async-start | bytes 1179648 | tf_op jit(solution)/shard_map/all_to_all | solution.py:332
  156.6 6.8 %collective-permute-start.22 = (f32[]{:T(128)}, f32[]{:T(128)}, u32[]{:S(2)}, u32[]{:S(2)}) collective-permute-start(f32[]{:T(128)} %bitcast.31), channel_id=1, source_target_pairs={{0,16},{16,0},{32,48},{48,32},{64,80},{80,64},{96,112},{112,96},{1... | collective-permute-start | bytes 20 | tf_op jit(solution)/shard_map/ppermute | solution.py:326
  163.4 3.8 %collective-permute-done.22 = f32[]{:T(128)} collective-permute-done((f32[]{:T(128)}, f32[]{:T(128)}, u32[]{:S(2)}, u32[]{:S(2)}) %collective-permute-start.22) | collective-permute-done | bytes 36 | tf_op jit(solution)/shard_map/ppermute | solution.py:326
  167.7 2.4 %collective-permute-start.23 = (f32[]{:T(128)}, f32[]{:T(128)}, u32[]{:S(2)}, u32[]{:S(2)}) collective-permute-start(f32[]{:T(128)} %add.214), channel_id=1, source_target_pairs={{0,32},{16,48},{32,0},{48,16},{64,96},{80,112},{96,64},{112,80},{1... | collective-permute-start | bytes 20 | tf_op jit(solution)/shard_map/ppermute | solution.py:326
  170.2 2.2 %collective-permute-done.23 = f32[]{:T(128)} collective-permute-done((f32[]{:T(128)}, f32[]{:T(128)}, u32[]{:S(2)}, u32[]{:S(2)}) %collective-permute-start.23) | collective-permute-done | bytes 36 | tf_op jit(solution)/shard_map/ppermute | solution.py:326
  172.9 5.8 %collective-permute-start.24 = (f32[]{:T(128)}, f32[]{:T(128)}, u32[]{:S(2)}, u32[]{:S(2)}) collective-permute-start(f32[]{:T(128)} %add.215), channel_id=1, source_target_pairs={{0,64},{16,80},{32,96},{48,112},{64,0},{80,16},{96,32},{112,48},{1... | collective-permute-start | bytes 20 | tf_op jit(solution)/shard_map/ppermute | solution.py:326
  178.7 1.8 collective-permute-done.24
  (74 shorter events, 16.4 us)
Async XLA Ops:
  7.2 17.2 %copy-start.3 = (s32[32]{0:T(128)S(1)}, s32[32]{0:T(128)}, u32[]{:S(2)}) copy-start(s32[32]{0:T(128)} %refs_1_.3) | copy-start | bytes 388
  7.2 73.3 %all-gather.2.cloned.1.call-start = ((), (), s32[]{:S(2)}) async-start(), calls=%async_computation.1 | async-start | bytes 2654208 | tf_op jit(solution)/shard_map/all_gather | solution.py:282
  8.3 4.3 %collective-permute-start.9 = (bf16[48,384]{1,0:T(8,128)(2,1)S(1)}, bf16[48,384]{1,0:T(8,128)(2,1)S(1)}, u32[]{:S(2)}, u32[]{:S(2)}) collective-permute-start(bf16[48,384]{1,0:T(8,128)(2,1)S(1)} %get-tuple-element.48), channel_id=1, source_target_pairs={{0,4},{4,0},{1,5},{5,1},{2,6},{6,2},{3,7},{7,3},{8,12},{12,8},{9,1... | collective-permute-start | bytes 110600 | tf_op jit(solution)/shard_map/ppermute | solution.py:35
  12.6 8.4 %collective-permute-start.12 = (bf16[96,384]{1,0:T(8,128)(2,1)S(1)}, bf16[96,384]{1,0:T(8,128)(2,1)S(1)}, u32[]{:S(2)}, u32[]{:S(2)}) collective-permute-start(bf16[96,384]{1,0:T(8,128)(2,1)S(1)} %maximum_select_fusion.3), channel_id=1, source_target_pairs={{0,136},{8,128},{128,8},{136,0},{1,137},{9,129},{129,9},{137,1},{2... | collective-permute-start | bytes 221192 | tf_op jit(solution)/shard_map/ppermute | solution.py:35
  17.2 5.9 %collective-permute-start.11 = (bf16[96,384]{1,0:T(8,128)(2,1)S(1)}, bf16[96,384]{1,0:T(8,128)(2,1)S(1)}, u32[]{:S(2)}, u32[]{:S(2)}) collective-permute-start(bf16[96,384]{1,0:T(8,128)(2,1)S(1)} %maximum_select_fusion.3), channel_id=1, source_target_pairs={{0,128},{128,0},{1,129},{129,1},{2,130},{130,2},{3,131},{131,3},{4... | collective-permute-start | bytes 221192 | tf_op jit(solution)/shard_map/ppermute | solution.py:35
  17.6 5.9 %collective-permute-start.10 = (bf16[96,384]{1,0:T(8,128)(2,1)S(1)}, bf16[96,384]{1,0:T(8,128)(2,1)S(1)}, u32[]{:S(2)}, u32[]{:S(2)}) collective-permute-start(bf16[96,384]{1,0:T(8,128)(2,1)S(1)} %maximum_select_fusion.3), channel_id=1, source_target_pairs={{0,8},{8,0},{1,9},{9,1},{2,10},{10,2},{3,11},{11,3},{4,12},{12,4},... | collective-permute-start | bytes 221192 | tf_op jit(solution)/shard_map/ppermute | solution.py:35
  27.8 31.1 %collective-permute-start.3 = (bf16[128,4608]{1,0:T(8,128)(2,1)}, bf16[128,4608]{1,0:T(8,128)(2,1)}, u32[]{:S(2)}, u32[]{:S(2)}) collective-permute-start(bf16[128,4608]{1,0:T(8,128)(2,1)} %get-tuple-element.23), channel_id=1, source_target_pairs={{0,4},{4,0},{1,5},{5,1},{2,6},{6,2},{3,7},{7,3},{8,12},{12,8},{9,1... | collective-permute-start | bytes 3538952 | tf_op jit(solution)/shard_map/ppermute | solution.py:35
  29.3 29.7 %collective-permute-start = (bf16[128,5376]{1,0:T(8,128)(2,1)}, bf16[128,5376]{1,0:T(8,128)(2,1)}, u32[]{:S(2)}, u32[]{:S(2)}) collective-permute-start(bf16[128,5376]{1,0:T(8,128)(2,1)} %get-tuple-element.21), channel_id=1, source_target_pairs={{0,2},{2,0},{1,3},{3,1},{4,6},{6,4},{5,7},{7,5},{8,10},{10,8},{9,1... | collective-permute-start | bytes 4128776 | tf_op jit(solution)/shard_map/ppermute | solution.py:35
  32.6 26.9 %collective-permute-start.13 = (bf16[768,768]{1,0:T(8,128)(2,1)S(1)}, bf16[768,768]{1,0:T(8,128)(2,1)S(1)}, u32[]{:S(2)}, u32[]{:S(2)}) collective-permute-start(bf16[768,768]{1,0:T(8,128)(2,1)S(1)} %pad_maximum_fusion), channel_id=1, source_target_pairs={{0,130},{2,128},{128,2},{130,0},{1,131},{3,129},{129,3},{131,1},{4... | collective-permute-start | bytes 3538952 | tf_op jit(solution)/shard_map/ppermute | solution.py:35
  34.8 29.0 %collective-permute-start.1 = (bf16[128,3840]{1,0:T(8,128)(2,1)S(1)}, bf16[128,3840]{1,0:T(8,128)(2,1)S(1)}, u32[]{:S(2)}, u32[]{:S(2)}) collective-permute-start(bf16[128,3840]{1,0:T(8,128)(2,1)S(1)} %copy-done.7), channel_id=1, source_target_pairs={{0,1},{1,0},{2,3},{3,2},{4,5},{5,4},{6,7},{7,6},{8,9},{9,8},{10,11... | collective-permute-start | bytes 2949128 | tf_op jit(solution)/shard_map/ppermute | solution.py:35
  58.9 21.6 %collective-permute-start.2 = (bf16[128,5376]{1,0:T(8,128)(2,1)}, bf16[128,5376]{1,0:T(8,128)(2,1)}, u32[]{:S(2)}, u32[]{:S(2)}) collective-permute-start(bf16[128,5376]{1,0:T(8,128)(2,1)} %collective-permute-done.refs_6_), channel_id=1, source_target_pairs={{0,1},{1,0},{2,3},{3,2},{4,5},{5,4},{6,7},{7,6},{8,9},{9,8},{10,11... | collective-permute-start | bytes 4128776 | tf_op jit(solution)/shard_map/ppermute | solution.py:35
  58.9 19.4 %collective-permute-start.6 = (bf16[128,4608]{1,0:T(8,128)(2,1)}, bf16[128,4608]{1,0:T(8,128)(2,1)}, u32[]{:S(2)}, u32[]{:S(2)}) collective-permute-start(bf16[128,4608]{1,0:T(8,128)(2,1)} %collective-permute-done.3.refs_9_), channel_id=1, source_target_pairs={{0,1},{1,0},{2,3},{3,2},{4,5},{5,4},{6,7},{7,6},{8,9},{9,8},{10,11... | collective-permute-start | bytes 3538952 | tf_op jit(solution)/shard_map/ppermute | solution.py:35
  60.6 19.9 %copy-start.8 = (s32[32]{0:T(128)S(1)}, s32[32]{0:T(128)}, u32[]{:S(2)}) copy-start(s32[32]{0:T(128)} %refs_2_.3) | copy-start | bytes 388
  60.6 19.9 %collective-permute-start.14 = (bf16[768,768]{1,0:T(8,128)(2,1)}, bf16[768,768]{1,0:T(8,128)(2,1)}, u32[]{:S(2)}, u32[]{:S(2)}) collective-permute-start(bf16[768,768]{1,0:T(8,128)(2,1)} %pad_maximum_fusion.1), channel_id=1, source_target_pairs={{0,1},{1,0},{2,3},{3,2},{4,5},{5,4},{6,7},{7,6},{8,9},{9,8},{10,11... | collective-permute-start | bytes 3538952 | tf_op jit(solution)/shard_map/ppermute | solution.py:35
  61.7 13.8 %collective-permute-start.5 = (bf16[64,3840]{1,0:T(8,128)(2,1)S(1)}, bf16[64,3840]{1,0:T(8,128)(2,1)}, u32[]{:S(2)}, u32[]{:S(2)}) collective-permute-start(bf16[64,3840]{1,0:T(8,128)(2,1)S(1)} %slice.77), channel_id=1, source_target_pairs={{0,2},{2,0},{1,3},{3,1},{4,6},{6,4},{5,7},{7,5},{8,10},{10,8},{9,1... | collective-permute-start | bytes 1474568 | tf_op jit(solution)/shard_map/ppermute | solution.py:35
  64.8 13.4 %collective-permute-start.4 = (bf16[64,3840]{1,0:T(8,128)(2,1)S(1)}, bf16[64,3840]{1,0:T(8,128)(2,1)}, u32[]{:S(2)}, u32[]{:S(2)}) collective-permute-start(bf16[64,3840]{1,0:T(8,128)(2,1)S(1)} %slice.76), channel_id=1, source_target_pairs={{0,4},{4,0},{1,5},{5,1},{2,6},{6,2},{3,7},{7,3},{8,12},{12,8},{9,1... | collective-permute-start | bytes 1474568 | tf_op jit(solution)/shard_map/ppermute | solution.py:35
  75.5 2.9 %collective-permute-start.8 = (bf16[64,3840]{1,0:T(8,128)(2,1)}, bf16[64,3840]{1,0:T(8,128)(2,1)}, u32[]{:S(2)}, u32[]{:S(2)}) collective-permute-start(bf16[64,3840]{1,0:T(8,128)(2,1)} %collective-permute-done.5.refs_11_), channel_id=1, source_target_pairs={{0,1},{1,0},{2,3},{3,2},{4,5},{5,4},{6,7},{7,6},{8,9},{9,8},{10,11... | collective-permute-start | bytes 1474568 | tf_op jit(solution)/shard_map/ppermute | solution.py:35
  78.3 2.2 %collective-permute-start.7 = (bf16[64,3840]{1,0:T(8,128)(2,1)}, bf16[64,3840]{1,0:T(8,128)(2,1)}, u32[]{:S(2)}, u32[]{:S(2)}) collective-permute-start(bf16[64,3840]{1,0:T(8,128)(2,1)} %collective-permute-done.4.refs_10_), channel_id=1, source_target_pairs={{0,1},{1,0},{2,3},{3,2},{4,5},{5,4},{6,7},{7,6},{8,9},{9,8},{10,11... | collective-permute-start | bytes 1474568 | tf_op jit(solution)/shard_map/ppermute | solution.py:35
  96.3 1.4 collective-permute-start.15
  98.9 7.5 %collective-permute-start.18 = (f32[1,1]{1,0:T(1,128)}, f32[1,1]{1,0:T(1,128)}, u32[]{:S(2)}, u32[]{:S(2)}) collective-permute-start(f32[1,1]{1,0:T(1,128)} %add.185), channel_id=1, source_target_pairs={{0,6},{2,4},{4,2},{6,0},{1,7},{3,5},{5,3},{7,1},{8,14},{10,12},{12... | collective-permute-start | bytes 20 | tf_op jit(solution)/shard_map/ppermute | solution.py:35
  101.5 5.4 %collective-permute-start.17 = (f32[1,1]{1,0:T(1,128)}, f32[1,1]{1,0:T(1,128)}, u32[]{:S(2)}, u32[]{:S(2)}) collective-permute-start(f32[1,1]{1,0:T(1,128)} %add.185), channel_id=1, source_target_pairs={{0,2},{2,0},{1,3},{3,1},{4,6},{6,4},{5,7},{7,5},{8,10},{10,8},{9,1... | collective-permute-start | bytes 20 | tf_op jit(solution)/shard_map/ppermute | solution.py:35
  104.1 3.6 %collective-permute-start.16 = (f32[1,1]{1,0:T(1,128)}, f32[1,1]{1,0:T(1,128)}, u32[]{:S(2)}, u32[]{:S(2)}) collective-permute-start(f32[1,1]{1,0:T(1,128)} %add.185), channel_id=1, source_target_pairs={{0,4},{4,0},{1,5},{5,1},{2,6},{6,2},{3,7},{7,3},{8,12},{12,8},{9,1... | collective-permute-start | bytes 20 | tf_op jit(solution)/shard_map/ppermute | solution.py:35
  112.7 18.1 %collective-permute-start.19 = (bf16[784,384]{1,0:T(8,128)(2,1)S(1)}, bf16[784,384]{1,0:T(8,128)(2,1)S(1)}, u32[]{:S(2)}, u32[]{:S(2)}) collective-permute-start(bf16[784,384]{1,0:T(8,128)(2,1)S(1)} %get-tuple-element.49), channel_id=1, source_target_pairs={{0,8},{8,0},{1,9},{9,1},{2,10},{10,2},{3,11},{11,3},{4,12},{12,4},... | collective-permute-start | bytes 1806344 | tf_op jit(solution)/shard_map/ppermute | solution.py:35
  114.6 25.2 %collective-permute-start.20 = (bf16[784,384]{1,0:T(8,128)(2,1)S(1)}, bf16[784,384]{1,0:T(8,128)(2,1)S(1)}, u32[]{:S(2)}, u32[]{:S(2)}) collective-permute-start(bf16[784,384]{1,0:T(8,128)(2,1)S(1)} %get-tuple-element.50), channel_id=1, source_target_pairs={{0,128},{128,0},{1,129},{129,1},{2,130},{130,2},{3,131},{131,3},{4... | collective-permute-start | bytes 1806344 | tf_op jit(solution)/shard_map/ppermute | solution.py:35
  116.9 25.4 %collective-permute-start.21 = (bf16[784,384]{1,0:T(8,128)(2,1)S(1)}, bf16[784,384]{1,0:T(8,128)(2,1)S(1)}, u32[]{:S(2)}, u32[]{:S(2)}) collective-permute-start(bf16[784,384]{1,0:T(8,128)(2,1)S(1)} %get-tuple-element.51), channel_id=1, source_target_pairs={{0,136},{8,128},{128,8},{136,0},{1,137},{9,129},{129,9},{137,1},{2... | collective-permute-start | bytes 1806344 | tf_op jit(solution)/shard_map/ppermute | solution.py:35
  146.1 35.1 %copy-start.9 = (f32[48,768]{1,0:T(8,128)S(1)}, f32[48,768]{1,0:T(8,128)}, u32[]{:S(2)}) copy-start(f32[48,768]{1,0:T(8,128)} %param.15) | copy-start | bytes 442372
  146.1 35.1 %copy-start.10 = (f32[48,768]{1,0:T(8,128)S(1)}, f32[48,768]{1,0:T(8,128)}, u32[]{:S(2)}) copy-start(f32[48,768]{1,0:T(8,128)} %param.16) | copy-start | bytes 442372
  146.1 35.1 %copy-start.11 = (f32[48,768]{1,0:T(8,128)S(1)}, f32[48,768]{1,0:T(8,128)}, u32[]{:S(2)}) copy-start(f32[48,768]{1,0:T(8,128)} %param.17) | copy-start | bytes 442372
  146.1 35.0 %all-to-all-start = ((bf16[16,48,384]{2,1,0:T(8,128)(2,1)}), bf16[16,48,384]{2,1,0:T(8,128)(2,1)S(1)}, u32[]{:S(2)}, u32[]{:S(2)}) async-start(bf16[16,48,384]{2,1,0:T(8,128)(2,1)} %bitcast.27), calls=%async_computation | async-start | bytes 1179648 | tf_op jit(solution)/shard_map/all_to_all | solution.py:332
  156.6 10.5 %collective-permute-start.22 = (f32[]{:T(128)}, f32[]{:T(128)}, u32[]{:S(2)}, u32[]{:S(2)}) collective-permute-start(f32[]{:T(128)} %bitcast.31), channel_id=1, source_target_pairs={{0,16},{16,0},{32,48},{48,32},{64,80},{80,64},{96,112},{112,96},{1... | collective-permute-start | bytes 20 | tf_op jit(solution)/shard_map/ppermute | solution.py:326
  167.7 4.6 %collective-permute-start.23 = (f32[]{:T(128)}, f32[]{:T(128)}, u32[]{:S(2)}, u32[]{:S(2)}) collective-permute-start(f32[]{:T(128)} %add.214), channel_id=1, source_target_pairs={{0,32},{16,48},{32,0},{48,16},{64,96},{80,112},{96,64},{112,80},{1... | collective-permute-start | bytes 20 | tf_op jit(solution)/shard_map/ppermute | solution.py:326
  172.9 7.6 %collective-permute-start.24 = (f32[]{:T(128)}, f32[]{:T(128)}, u32[]{:S(2)}, u32[]{:S(2)}) collective-permute-start(f32[]{:T(128)} %add.215), channel_id=1, source_target_pairs={{0,64},{16,80},{32,96},{48,112},{64,0},{80,16},{96,32},{112,48},{1... | collective-permute-start | bytes 20 | tf_op jit(solution)/shard_map/ppermute | solution.py:326
  (7 other events, 60.6 us)
Sparse Core Ops, SparseCore 0:
  24.3 43.5 all-gather.1

commit v3 on v2

--- a/solution.py
+++ b/solution.py
@@ -49,7 +49,7 @@
     )
 
 
-def pack_kernel(half, at, timestep, latents, noise, gain, feats, send_y, send_x, send_c):
+def pack_kernel(half, at, timestep, latents, noise, gain, feats, send, send_y, send_x, send_c):
     time = (timestep[at[0]].astype(f32) + 0.5) / STEPS
     clean, drawn = latents[...].astype(f32), noise[...].astype(f32)
     value = normalize((1.0 - time) * clean + time * drawn, gain[...])
@@ -57,30 +57,25 @@
     low, high = value[:, : width // 2], value[:, width // 2 :]
     value = jnp.where(at[1] == 0, value, jnp.concatenate([high, low], 1))
 
-    def fill(out, places, after_feats):
-        col = 0
-        for array, place in places:
+    def fill(out, places, feats_at=None):
+        for col, (array, place) in enumerate(places):
             start = pl.multiple_of(at[place] * half, 128)
+            col = col * half + (width if feats_at == 0 else 0)
             out[:, col : col + half] = array[:, pl.ds(start, half)]
-            col += half
-        out[:, col : col + width] = value
-        col += width
-        for array, place in after_feats:
-            start = pl.multiple_of(at[place] * half, 128)
-            out[:, col : col + half] = array[:, pl.ds(start, half)]
-            col += half
-
-    diagonal = [(latents, 8), (latents, 7)]
+        if feats_at is not None:
+            out[:, feats_at * half : feats_at * half + width] = value
+
     feats[...] = value
-    fill(send_y, [(latents, 3), (noise, 3), (latents, 4), (noise, 4)], diagonal)
-    fill(send_x, [(latents, 5), (latents, 6)], diagonal)
-    fill(send_c, [(latents, 2), (noise, 2)], [])
+    fill(send, [(latents, 8), (latents, 7)], 0)
+    fill(send_y, [(latents, 3), (noise, 3), (latents, 4), (noise, 4)])
+    fill(send_x, [(latents, 5), (latents, 6)])
+    fill(send_c, [(latents, 2), (noise, 2)], 2)
 
 
 def pack(at, timestep, latents, noise, gain, half):
     tok, width = latents.shape
     rows = tok // 4
-    widths = (width, width + 6 * half, width + 4 * half, width + 2 * half)
+    widths = (width, width + 2 * half, 4 * half, 2 * half, width + 2 * half)
     small = pl.BlockSpec(memory_space=pltpu.SMEM)
     return pl.pallas_call(
         lambda *refs: pack_kernel(half, *refs),
@@ -94,7 +89,7 @@
         ],
         out_specs=[pl.BlockSpec((rows, w), lambda i: (i, 0)) for w in widths],
         out_shape=[jax.ShapeDtypeStruct((tok, w), bf16) for w in widths],
-        compiler_params=pltpu.CompilerParams(vmem_limit_bytes=16 * 2**20),
+        compiler_params=pltpu.CompilerParams(vmem_limit_bytes=56 * 2**20),
         cost_estimate=pl.CostEstimate(
             flops=20 * tok * width, bytes_accessed=15 * tok * width, transcendentals=tok * width
         ),
@@ -103,8 +98,9 @@
 
 
 def project_kernel(
-    half, at, timestep, winner, latents, noise, feats, got_y, got_c, got_yc, got_x, diag_0, diag_1,
-    got_xc, diag_c0, diag_c1, policy, reference, ref_y, ref_c, gap, near, near_x, far, far_x,
+    half, at, timestep, winner, latents, noise, feats, rows_y, rows_yc, rows_x, rows_xc, got_c,
+    got_y, got_yc, got_x, got_xc, diag_0, diag_1, diag_c0, diag_c1, policy, reference, ref_y, ref_c,
+    gap, near, near_x, far, far_x,
     rows_ref, both, clean, drawn, grad, sems,
 ):
     tok, width = feats.shape
@@ -144,13 +140,13 @@
         target = both.at[pl.ds(pl.multiple_of(place, block), block), lanes(1)]
         weight_copies.append(start(source, target))
 
-    def piece(k, source, feats_at, clean_at, drawn_at):
+    def piece(k, source, feats_at, beside, clean_at, drawn_at):
         copies = [
             start(source.at[:, lanes(feats_at, width)], rows_ref.at[rows_of(k)]),
-            start(source.at[:, lanes(clean_at)], clean.at[rows_of(k)]),
+            start(beside.at[:, lanes(clean_at)], clean.at[rows_of(k)]),
         ]
         if drawn_at is not None:
-            copies.append(start(source.at[:, lanes(drawn_at)], drawn.at[rows_of(k)]))
+            copies.append(start(beside.at[:, lanes(drawn_at)], drawn.at[rows_of(k)]))
         return copies
 
     def halves(k, source):
@@ -167,10 +163,10 @@
             start(latents.at[:, mine], clean.at[rows_of(0)]),
             start(noise.at[:, mine], drawn.at[rows_of(0)]),
         ]
-        + piece(1, got_y, 4, 0, 1),
-        piece(2, got_c, 2, 0, 1) + piece(3, got_yc, 4, 2, 3),
-        piece(4, got_x, 2, 0, None) + halves(5, (diag_0, diag_1)),
-        piece(6, got_xc, 2, 1, None) + halves(7, (diag_c0, diag_c1)),
+        + piece(1, rows_y, 0, got_y, 0, 1),
+        piece(2, got_c, 2, got_c, 0, 1) + piece(3, rows_yc, 0, got_yc, 2, 3),
+        piece(4, rows_x, 0, got_x, 0, None) + halves(5, (diag_0, diag_1)),
+        piece(6, rows_xc, 0, got_xc, 1, None) + halves(7, (diag_c0, diag_c1)),
     ]
     for copy in weight_copies:
         copy.wait()
@@ -213,7 +209,7 @@
 
 def project(at, timestep, winner, half, *arrays):
     tok, width = arrays[2].shape
-    policy = arrays[12]
+    policy = arrays[16]
     out_rows = policy.shape[0] * policy.shape[2] // 2 + 16
     small = pl.BlockSpec(memory_space=pltpu.SMEM)
     block = jax.ShapeDtypeStruct((out_rows, half), bf16)
@@ -230,12 +226,60 @@
             pltpu.VMEM((8 * tok, half), bf16),
             pltpu.SemaphoreType.DMA((48,)),
         ],
-        compiler_params=pltpu.CompilerParams(vmem_limit_bytes=40 * 2**20),
+        compiler_params=pltpu.CompilerParams(vmem_limit_bytes=56 * 2**20),
         cost_estimate=pl.CostEstimate(
             flops=6 * 8 * tok * width * half, bytes_accessed=16 * 2**20, transcendentals=0
         ),
         name="project",
     )(at, timestep, winner, *arrays)
+
+
+def stamp_kernel(scale, gap, gap_x, gap_y, gap_d, margin, terms):
+    total = gap_x[...] + gap_y[...] + (gap_d[...] + gap[...])
+    value = -0.5 * BETA * (total / scale)
+    margin[...] = value
+    value = value[:1, :1]
+    first = value.astype(bf16).astype(f32)
+    second = (value - first).astype(bf16).astype(f32)
+    third = (value - first) - second
+    row = lax.broadcasted_iota(jnp.int32, terms.shape, 0)
+    rest = jnp.where(row == 2, third, 0.0)
+    terms[...] = jnp.where(row == 0, first, jnp.where(row == 1, second, rest)).astype(bf16)
+
+
+def stamp(scale, half, *gaps):
+    return pl.pallas_call(
+        lambda *refs: stamp_kernel(scale, *refs),
+        out_shape=[
+            jax.ShapeDtypeStruct(gaps[0].shape, f32),
+            jax.ShapeDtypeStruct((16, half), bf16),
+        ],
+        name="stamp",
+    )(*gaps)
+
+
+def combine_kernel(factor, margin, near, got_x, got_y, got_d, out):
+    size = out.shape[0]
+
+    def weight(value):
+        return (jax.nn.sigmoid(-value) * factor)[:1, :1]
+
+    total = weight(margin[...]) * near[:size, :].astype(f32)
+    for block in (got_x, got_y, got_d):
+        terms = block[size : size + 16, :128].astype(f32)
+        value = (terms[0:1] + terms[1:2]) + terms[2:3]
+        total = total + weight(value) * block[:size, :].astype(f32)
+    out[...] = total.astype(bf16)
+
+
+def combine(factor, margin, *blocks):
+    rows, half = blocks[0].shape
+    return pl.pallas_call(
+        lambda *refs: combine_kernel(factor, *refs),
+        out_shape=jax.ShapeDtypeStruct((rows - 16, half), bf16),
+        compiler_params=pltpu.CompilerParams(vmem_limit_bytes=24 * 2**20),
+        name="combine",
+    )(margin, *blocks)
 
 
 def body(
@@ -254,80 +298,67 @@
     policy_bf = policy_master.astype(bf16)
     own_w = lax.dynamic_slice_in_dim(policy_bf, xl * half, half, 1)
     other_w = flip(lax.dynamic_slice_in_dim(policy_bf, (1 - xl) * half, half, 1), "xl")
-    own_w = ordered(xl, own_w, other_w)
-    same_z = jnp.stack(
-        [
-            ordered(xh, own_w[None], flip(own_w, "xh")[None]),
-            ordered(xh, flip(own_w, "yh")[None], flip(own_w, "yh", "xh")[None]),
-        ]
-    )[:, None]
-
     blocks = [
         ((yl ^ dy) * 2 + (c ^ dc)) * 2 + (xl ^ dx)
         for dx, dy in ((0, 0), (0, 1), (1, 0), (1, 1))
         for dc in (0, 1)
     ]
     at = jnp.stack([pair, yh] + blocks[1:])
-    feats, send_y, send_x, send_c = pack(at, timestep, latents, noise, norm_gain, half)
-    send_y, send_x, send_c, weight_in, _ = lax.optimization_barrier(
-        (send_y, send_x, send_c, reference_weight, same_z)
-    )
-    got_y, got_x, got_c = flip(send_y, "yl"), flip(send_x, "xl"), flip(send_c, "c")
+    feats, send, send_y, send_x, send_c = pack(at, timestep, latents, noise, norm_gain, half)
+    own_w = ordered(xl, own_w, other_w)
+    same_z = jnp.stack(
+        [
+            ordered(xh, own_w[None], after(flip(own_w, "xh"), feats)[None]),
+            ordered(xh, flip(own_w, "yh")[None], flip(own_w, "yh", "xh")[None]),
+        ]
+    )[:, None]
+
+    send, send_c, weight_in, _ = lax.optimization_barrier((send, send_c, reference_weight, same_z))
+    rows_y, rows_x, got_c = flip(send, "yl"), flip(send, "xl"), flip(send_c, "c")
+    send_y, send_x, rows_y, rows_x = lax.optimization_barrier((send_y, send_x, rows_y, rows_x))
+    got_y, got_x = flip(send_y, "yl"), flip(send_x, "xl")
 
     ref_y = flip(
         jnp.concatenate([columns(weight_in, 0, 1, 0), columns(weight_in, 0, 1, 1)], 1), "yh", "yl"
     )
+    ref_y = after(ref_y, got_y)
     ref_c = flip(jnp.concatenate([columns(weight_in, 0, 0, 1), ref_y[:, half:]], 1), "c")
+
     n_z = SIZES[1]
     per_z = lax.all_gather(same_z.reshape(-1, half), "z").reshape(n_z, 2, -1, half)
 
     h = tok // 2
-    diag = [flip(got_y[:h, 4 * half :], "xl"), flip(got_x[h:, 2 * half :], "yl")]
+    diag = [flip(rows_y[:h], "xl"), flip(rows_x[h:], "yl")]
     diag_c = [flip(part, "c") for part in diag]
+    rows_yc, rows_xc = flip(rows_y, "c"), flip(rows_x, "c")
     got_yc, got_xc = flip(got_y, "c"), flip(got_x, "c")
 
     places = jnp.stack([pair, yh, yl, c, xh, xl, blocks[0]])
     gap, near, near_x, far, far_x = project(
-        places, timestep, winner, half, latents, noise, feats, got_y, got_c, got_yc, got_x,
-        *diag, got_xc, *diag_c, per_z, reference_weight, ref_y, ref_c,
-    )
-
-    gap = gap[:1, :1]
+        places, timestep, winner, half, latents, noise, feats, rows_y, rows_yc, rows_x, rows_xc,
+        got_c, got_y, got_yc, got_x, got_xc, *diag, *diag_c, per_z, reference_weight, ref_y, ref_c,
+    )
+
     gap = gap + flip(gap, "c")
-    gap = flip(gap, "xl") + flip(gap, "yl") + (flip(gap, "xl", "yl") + gap)
-    margin = -0.5 * BETA * (gap / scale)
-    first = lax.reduce_precision(margin, 8, 7)
-    second = lax.reduce_precision(margin - first, 8, 7)
-    terms = jnp.concatenate([first, second, (margin - first) - second]).astype(bf16)
-    terms = jnp.broadcast_to(jnp.concatenate([terms, jnp.zeros((13, 1), bf16)]), (16, half))
+    margin, terms = stamp(
+        scale, half, gap, flip(gap, "xl"), flip(gap, "yl"), flip(gap, "xl", "yl")
+    )
     size = near.shape[0] - 16
 
     def with_margin(block):
         return lax.dynamic_update_slice(block, terms, (size, 0))
 
-    got = [
-        near,
-        flip(with_margin(near_x), "xh"),
-        flip(with_margin(far), "yh"),
-        flip(with_margin(far_x), "yh", "xh"),
-    ]
-
-    def margin_of(block):
-        first, second, third = (block[size + i : size + i + 1, :1].astype(f32) for i in range(3))
-        return (first + second) + third
-
-    margins = [margin] + [margin_of(g) for g in got[1:]]
-    weights = [
-        jax.nn.sigmoid(-m) * BETA / (2.0 * count_pairs) * (2.0 / scale) for m in margins
-    ]
-    losses = [jax.nn.softplus(-m) for m in margins]
-    loss = ((losses[0] + losses[1]) + (losses[2] + losses[3])).reshape(())
+    got_x = flip(with_margin(near_x), "xh")
+    got_y = flip(with_margin(far), "yh")
+    got_d = flip(with_margin(far_x), "yh", "xh")
+    loss = jax.nn.softplus(-margin[0, 0])
     for step in (1, 2, 4):
         loss = loss + lax.ppermute(loss, "z", [(i, i ^ step) for i in range(n_z)])
+    factor = BETA / (2.0 * count_pairs) * (2.0 / scale)
+    summed = combine(factor, after(margin, loss), near, got_x, got_y, got_d)
+    loss = after(loss, summed)
+    loss = (loss + flip(loss, "xh")) + (flip(loss, "yh") + flip(loss, "yh", "xh"))
     loss = loss / count_pairs
-    got = [g[:size] for g in got]
-
-    summed = sum(w * g.astype(f32) for w, g in zip(weights, got)).astype(bf16)
     rows = policy_master.shape[0]
     blocks = lax.all_to_all(
         summed.reshape(-1, rows, half), ("z", "xl"), split_axis=0, concat_axis=0, tiled=True

time: 191 us -> 181 us (0.948)
  waiting for transfers between devices: 72.4 us -> 56.4 us
  between operations: 30.3 us -> 19.7 us
  starting transfers between devices: 56.1 us -> 65.8 us
  Pallas kernels: 17.5 us -> 23.5 us
  local copies, waits for them, and re-layouts: 8.36 us -> 11.2 us
    ppermute x22 -> x29, waiting for transfers between devices: 64.6 us -> 51.1 us  [flip(): return lax.ppermute(x, axes, [(i, last - i) for i in range(last + 1)])]
    ppermute x22 -> x29, starting transfers between devices: 31 us -> 39.4 us  [flip(): return lax.ppermute(x, axes, [(i, last - i) for i in range(last + 1)])]
    ppermute x3, waiting for transfers between devices: 7.77 us -> 1.08 us  [body(): loss = loss + lax.ppermute(loss, 'z', [(i, i ^ step) for i in range(n_z)])]
    all_to_all x1, waiting for transfers between devices: 0.01 us -> 4.16 us  [body(): lax.all_to_all(summed.reshape(-1, rows, half), ('z', 'xl'), split_axis=0,...]
    pallas_call x0 -> x2, Pallas kernels: none -> 3.25 us  [the longest x1 1.88 us: combine(): pl.pallas_call(lambda *refs: combine_kernel(factor, *refs), out_shape=jax...]
    unnamed x24 -> x42, local copies, waits for them, and re-layouts: 2.18 us -> 4.63 us
    slice x6 -> x3, local copies, waits for them, and re-layouts: 4.23 us -> 2.28 us  [the longest x1 1.18 us: body(): loss = jax.nn.softplus(-margin[0, 0])]
  transfers between devices with their start and end apart: 27 -> 34, of which waited for: 15 -> 21; matrix products, arithmetic and copies ran while one was open for 3% -> 3% of each run, Pallas kernels for 2% -> 3%
where the time goes in v3:
time: 181 us; the launch traced here: 180 us
  starting transfers between devices  65.8 us (36%)
  waiting for transfers between devices  56.4 us (31%)
  Pallas kernels  23.5 us (13%)
  between operations  19.7 us (11%)
  local copies, waits for them, and re-layouts  11.2 us (6%)
  other arithmetic  3.54 us (2%)
    ppermute x29, waiting for transfers between devices, flip(): return lax.ppermute(x, axes, [(i, last - i) for i in range(last + 1)])  51.1 us
    ppermute x29, starting transfers between devices, flip(): return lax.ppermute(x, axes, [(i, last - i) for i in range(last + 1)])  39.4 us
    ppermute x3, starting transfers between devices, body(): loss = loss + lax.ppermute(loss, 'z', [(i, i ^ step) for i in range(n_z)])  16.2 us
    pallas_call x1, Pallas kernels, project(): pl.pallas_call(lambda *refs: project_kernel(half, *refs), in_specs=[small...  15.6 us
    all_to_all x1, starting transfers between devices, body(): lax.all_to_all(summed.reshape(-1, rows, half), ('z', 'xl'), split_axis=0,...  10.2 us
    unnamed x42, local copies, waits for them, and re-layouts  4.63 us
    pallas_call x1, Pallas kernels, pack(): pl.pallas_call(lambda *refs: pack_kernel(half, *refs), grid=(tok // rows,...  4.62 us
    all_to_all x1, waiting for transfers between devices, body(): lax.all_to_all(summed.reshape(-1, rows, half), ('z', 'xl'), split_axis=0,...  4.16 us
  transfers between devices with their start and end apart: 34, of which 21 were waited for; matrix products, arithmetic and copies ran while one was open for 3% of the time, Pallas kernels for 3%

profile of v3, /device:TPU:2, one launch (start us, length us, event | category | flops | bytes accessed | tf_op | source)
XLA Modules:
  0.0 180.2 jit_solution(8749063760656379146)
XLA Ops:
  8.2 2.4 %collective-permute-start.13 = (bf16[48,384]{1,0:T(8,128)(2,1)S(1)}, bf16[48,384]{1,0:T(8,128)(2,1)S(1)}, u32[]{:S(2)}, u32[]{:S(2)}) collective-permute-start(bf16[48,384]{1,0:T(8,128)(2,1)S(1)} %get-tuple-element.59), channel_id=1, source_target_pairs={{0,4},{4,0},{1,5},{5,1},{2,6},{6,2},{3,7},{7,3},{8,12},{12,8},{9,1... | collective-permute-start | bytes 110600 | tf_op jit(solution)/shard_map/ppermute | solution.py:35
  11.1 4.6 %pack.1 = (bf16[128,3072]{1,0:T(8,128)(2,1)}, bf16[128,3840]{1,0:T(8,128)(2,1)}, bf16[128,1536]{1,0:T(8,128)(2,1)}, bf16[128,768]{1,0:T(8,128)(2,1)}, bf16[128,3840]{1,0:T(8,128)(2,1)}) custom-call(s32[9]{0:T(128)} %stack.70.refs_0_, s32[32]{0:T(128)} %refs_1_.3, bf16[128,3072]{1,0:T(8,128)(2,1)} %refs_3_.3, bf16[128,3072]{1,0:T(8,128)(2,1)} %refs_4_.1, ...), custom_call_target="tpu_custom_call" | custom-call | flops 7864320 | bytes 5898240 | tf_op jit(solution)/shard_map/pack/pallas_call | solution.py:80
  15.8 3.4 %collective-permute-start.16 = (bf16[96,384]{1,0:T(8,128)(2,1)S(1)}, bf16[96,384]{1,0:T(8,128)(2,1)S(1)}, u32[]{:S(2)}, u32[]{:S(2)}) collective-permute-start(bf16[96,384]{1,0:T(8,128)(2,1)S(1)} %maximum_select_fusion.3), channel_id=1, source_target_pairs={{0,136},{8,128},{128,8},{136,0},{1,137},{9,129},{129,9},{137,1},{2... | collective-permute-start | bytes 221192 | tf_op jit(solution)/shard_map/ppermute | solution.py:35
  19.5 2.8 %collective-permute-start.14 = (bf16[96,384]{1,0:T(8,128)(2,1)S(1)}, bf16[96,384]{1,0:T(8,128)(2,1)S(1)}, u32[]{:S(2)}, u32[]{:S(2)}) collective-permute-start(bf16[96,384]{1,0:T(8,128)(2,1)S(1)} %maximum_select_fusion.3), channel_id=1, source_target_pairs={{0,8},{8,0},{1,9},{9,1},{2,10},{10,2},{3,11},{11,3},{4,12},{12,4},... | collective-permute-start | bytes 221192 | tf_op jit(solution)/shard_map/ppermute | solution.py:35
  22.4 3.0 %collective-permute-done.14 = bf16[96,384]{1,0:T(8,128)(2,1)S(1)} collective-permute-done((bf16[96,384]{1,0:T(8,128)(2,1)S(1)}, bf16[96,384]{1,0:T(8,128)(2,1)S(1)}, u32[]{:S(2)}, u32[]{:S(2)}) %collective-permute-start.14) | collective-permute-done | bytes 73760 | tf_op jit(solution)/shard_map/ppermute | solution.py:35
  26.2 1.9 %collective-permute-start.1 = (bf16[128,3840]{1,0:T(8,128)(2,1)S(1)}, bf16[128,3840]{1,0:T(8,128)(2,1)S(1)}, u32[]{:S(2)}, u32[]{:S(2)}) collective-permute-start(bf16[128,3840]{1,0:T(8,128)(2,1)S(1)} %copy-done.13), channel_id=1, source_target_pairs={{0,4},{4,0},{1,5},{5,1},{2,6},{6,2},{3,7},{7,3},{8,12},{12,8},{9,1... | collective-permute-start | bytes 2949128 | tf_op jit(solution)/shard_map/ppermute | solution.py:35
  28.1 1.6 collective-permute-start
  29.7 1.6 constant_dynamic-slice_fusion
  31.4 2.3 %collective-permute-start.17 = (bf16[768,768]{1,0:T(8,128)(2,1)S(1)}, bf16[768,768]{1,0:T(8,128)(2,1)S(1)}, u32[]{:S(2)}, u32[]{:S(2)}) collective-permute-start(bf16[768,768]{1,0:T(8,128)(2,1)S(1)} %pad_maximum_fusion), channel_id=1, source_target_pairs={{0,130},{2,128},{128,2},{130,0},{1,131},{3,129},{129,3},{131,1},{4... | collective-permute-start | bytes 3538952 | tf_op jit(solution)/shard_map/ppermute | solution.py:35
  33.7 14.4 %collective-permute-done.1.refs_8_ = bf16[128,3840]{1,0:T(8,128)(2,1)S(1)} collective-permute-done((bf16[128,3840]{1,0:T(8,128)(2,1)S(1)}, bf16[128,3840]{1,0:T(8,128)(2,1)S(1)}, u32[]{:S(2)}, u32[]{:S(2)}) %collective-permute-start.1) | collective-permute-done | bytes 983072 | tf_op jit(solution)/shard_map/ppermute | solution.py:35
  48.1 1.9 %collective-permute-done.refs_6_ = bf16[128,3840]{1,0:T(8,128)(2,1)} collective-permute-done((bf16[128,3840]{1,0:T(8,128)(2,1)S(1)}, bf16[128,3840]{1,0:T(8,128)(2,1)}, u32[]{:S(2)}, u32[]{:S(2)}) %collective-permute-start) | collective-permute-done | bytes 983072 | tf_op jit(solution)/shard_map/ppermute | solution.py:35
  50.0 1.6 collective-permute-start.5
  52.4 4.9 %collective-permute-done.7.refs_13_ = bf16[128,768]{1,0:T(8,128)(2,1)S(1)} collective-permute-done((bf16[128,768]{1,0:T(8,128)(2,1)S(1)}, bf16[128,768]{1,0:T(8,128)(2,1)S(1)}, u32[]{:S(2)}, u32[]{:S(2)}) %collective-permute-start.7) | collective-permute-done | bytes 196640 | tf_op jit(solution)/shard_map/ppermute | solution.py:35
  57.9 4.2 %collective-permute-done.5.refs_11_ = bf16[128,1536]{1,0:T(8,128)(2,1)S(1)} collective-permute-done((bf16[128,1536]{1,0:T(8,128)(2,1)S(1)}, bf16[128,1536]{1,0:T(8,128)(2,1)S(1)}, u32[]{:S(2)}, u32[]{:S(2)}) %collective-permute-start.5) | collective-permute-done | bytes 393248 | tf_op jit(solution)/shard_map/ppermute | solution.py:35
  64.9 3.6 %collective-permute-done.10.refs_16_ = bf16[64,3840]{1,0:T(8,128)(2,1)} collective-permute-done((bf16[64,3840]{1,0:T(8,128)(2,1)S(1)}, bf16[64,3840]{1,0:T(8,128)(2,1)}, u32[]{:S(2)}, u32[]{:S(2)}) %collective-permute-start.10) | collective-permute-done | bytes 491552 | tf_op jit(solution)/shard_map/ppermute | solution.py:35
  68.4 8.9 %collective-permute-done.9.refs_15_ = bf16[64,3840]{1,0:T(8,128)(2,1)} collective-permute-done((bf16[64,3840]{1,0:T(8,128)(2,1)S(1)}, bf16[64,3840]{1,0:T(8,128)(2,1)}, u32[]{:S(2)}, u32[]{:S(2)}) %collective-permute-start.9) | collective-permute-done | bytes 491552 | tf_op jit(solution)/shard_map/ppermute | solution.py:35
  81.3 15.6 %project.1 = (f32[8,128]{1,0:T(8,128)}, bf16[784,384]{1,0:T(8,128)(2,1)}, bf16[784,384]{1,0:T(8,128)(2,1)}, bf16[784,384]{1,0:T(8,128)(2,1)}, bf16[784,384]{1,0:T(8,128)(2,1)}) custom-call(s32[7]{0:T(128)} %stack.62.refs_0_, s32[32]{0:T(128)} %refs_1_.3, s32[32]{0:T(128)} %refs_2_.3, bf16[128,3072]{1,0:T(8,128)(2,1)} %refs_3_.3, bf16[128,3072]{1,0:T(8,128)(2,1)} %refs_4_.1, ...), custom_call_target="tpu_custom_call" | custom-call | flops 7247757312 | bytes 16777216 | tf_op jit(solution)/shard_map/project/pallas_call | solution.py:216
  100.9 1.7 collective-permute-start.20
  105.2 1.4 stamp.1
  107.9 3.6 %collective-permute-start.28 = (bf16[784,384]{1,0:T(8,128)(2,1)}, bf16[784,384]{1,0:T(8,128)(2,1)S(1)}, u32[]{:S(2)}, u32[]{:S(2)}) collective-permute-start(bf16[784,384]{1,0:T(8,128)(2,1)} %get-tuple-element.60), channel_id=1, source_target_pairs={{0,136},{8,128},{128,8},{136,0},{1,137},{9,129},{129,9},{137,1},{2... | collective-permute-start | bytes 1806344 | tf_op jit(solution)/shard_map/ppermute | solution.py:35
  112.0 2.5 %collective-permute-start.26 = (bf16[784,384]{1,0:T(8,128)(2,1)}, bf16[784,384]{1,0:T(8,128)(2,1)S(1)}, u32[]{:S(2)}, u32[]{:S(2)}) collective-permute-start(bf16[784,384]{1,0:T(8,128)(2,1)} %get-tuple-element.62), channel_id=1, source_target_pairs={{0,8},{8,0},{1,9},{9,1},{2,10},{10,2},{3,11},{11,3},{4,12},{12,4},... | collective-permute-start | bytes 1806344 | tf_op jit(solution)/shard_map/ppermute | solution.py:35
  116.4 3.3 %collective-permute-start.23 = (f32[]{:T(128)}, f32[]{:T(128)}, u32[]{:S(2)}, u32[]{:S(2)}) collective-permute-start(f32[]{:T(128)} %select_n.85), channel_id=1, source_target_pairs={{0,16},{16,0},{32,48},{48,32},{64,80},{80,64},{96,112},{112,96},{1... | collective-permute-start | bytes 20 | tf_op jit(solution)/shard_map/ppermute | solution.py:356
  120.7 4.6 %collective-permute-start.24 = (f32[]{:T(128)}, f32[]{:T(128)}, u32[]{:S(2)}, u32[]{:S(2)}) collective-permute-start(f32[]{:T(128)} %add.128), channel_id=1, source_target_pairs={{0,32},{16,48},{32,0},{48,16},{64,96},{80,112},{96,64},{112,80},{1... | collective-permute-start | bytes 20 | tf_op jit(solution)/shard_map/ppermute | solution.py:356
  126.2 8.2 %collective-permute-start.25 = (f32[]{:T(128)}, f32[]{:T(128)}, u32[]{:S(2)}, u32[]{:S(2)}) collective-permute-start(f32[]{:T(128)} %add.129), channel_id=1, source_target_pairs={{0,64},{16,80},{32,96},{48,112},{64,0},{80,16},{96,32},{112,48},{1... | collective-permute-start | bytes 20 | tf_op jit(solution)/shard_map/ppermute | solution.py:356
  135.3 4.0 %collective-permute-done.27.refs_3_ = bf16[784,384]{1,0:T(8,128)(2,1)S(1)} collective-permute-done((bf16[784,384]{1,0:T(8,128)(2,1)}, bf16[784,384]{1,0:T(8,128)(2,1)S(1)}, u32[]{:S(2)}, u32[]{:S(2)}) %collective-permute-start.27) | collective-permute-done | bytes 602144 | tf_op jit(solution)/shard_map/ppermute | solution.py:35
  141.3 1.9 %combine.1 = bf16[768,384]{1,0:T(8,128)(2,1)} custom-call(f32[8,128]{1,0:T(8,128)S(1)} %copy-done.1, bf16[784,384]{1,0:T(8,128)(2,1)S(1)} %copy-done, bf16[784,384]{1,0:T(8,128)(2,1)S(1)} %collective-permute-done.26.refs_2_, bf16[784,384]{1,0:T(8,128)(2,1)S(1)} %collective-permute-done.27.refs_3_, bf16[784,384]{1,0:T(8,128)(2,1)S(1)} %collective-permute-done.28.refs_4_), custom_call_target="tpu_custom_call" | custom-call | tf_op jit(solution)/shard_map/combine/pallas_call | solution.py:277
  143.2 10.2 %all-to-all-start = ((bf16[16,48,384]{2,1,0:T(8,128)(2,1)}), bf16[16,48,384]{2,1,0:T(8,128)(2,1)S(1)}, u32[]{:S(2)}, u32[]{:S(2)}) async-start(bf16[16,48,384]{2,1,0:T(8,128)(2,1)} %bitcast.24), calls=%async_computation | async-start | bytes 1179648 | tf_op jit(solution)/shard_map/all_to_all | solution.py:363
  153.4 4.3 %collective-permute-start.31 = (f32[]{:T(128)}, f32[]{:T(128)}, u32[]{:S(2)}, u32[]{:S(2)}) collective-permute-start(f32[]{:T(128)} %add.130), channel_id=1, source_target_pairs={{0,136},{8,128},{128,8},{136,0},{1,137},{9,129},{129,9},{137,1},{2... | collective-permute-start | bytes 20 | tf_op jit(solution)/shard_map/ppermute | solution.py:35
  157.7 2.3 %collective-permute-start.30 = (f32[]{:T(128)}, f32[]{:T(128)}, u32[]{:S(2)}, u32[]{:S(2)}) collective-permute-start(f32[]{:T(128)} %add.130), channel_id=1, source_target_pairs={{0,128},{128,0},{1,129},{129,1},{2,130},{130,2},{3,131},{131,3},{4... | collective-permute-start | bytes 20 | tf_op jit(solution)/shard_map/ppermute | solution.py:35
  160.0 3.8 %collective-permute-start.29 = (f32[]{:T(128)}, f32[]{:T(128)}, u32[]{:S(2)}, u32[]{:S(2)}) collective-permute-start(f32[]{:T(128)} %add.130), channel_id=1, source_target_pairs={{0,8},{8,0},{1,9},{9,1},{2,10},{10,2},{3,11},{11,3},{4,12},{12,4},... | collective-permute-start | bytes 20 | tf_op jit(solution)/shard_map/ppermute | solution.py:35
  163.8 1.4 collective-permute-done.29
  167.1 4.2 %all-to-all-done = bf16[16,48,384]{2,1,0:T(8,128)(2,1)S(1)} async-done(((bf16[16,48,384]{2,1,0:T(8,128)(2,1)}), bf16[16,48,384]{2,1,0:T(8,128)(2,1)S(1)}, u32[]{:S(2)}, u32[]{:S(2)}) %all-to-all-start) | async-done | bytes 589856 | tf_op jit(solution)/shard_map/all_to_all | solution.py:363
  (104 shorter events, 24.5 us)
Async XLA Ops:
  7.2 73.3 %all-gather.2.cloned.1.call-start = ((), (), s32[]{:S(2)}) async-start(), calls=%async_computation.1 | async-start | bytes 2654208 | tf_op jit(solution)/shard_map/all_gather | solution.py:328
  8.2 7.6 %collective-permute-start.13 = (bf16[48,384]{1,0:T(8,128)(2,1)S(1)}, bf16[48,384]{1,0:T(8,128)(2,1)S(1)}, u32[]{:S(2)}, u32[]{:S(2)}) collective-permute-start(bf16[48,384]{1,0:T(8,128)(2,1)S(1)} %get-tuple-element.59), channel_id=1, source_target_pairs={{0,4},{4,0},{1,5},{5,1},{2,6},{6,2},{3,7},{7,3},{8,12},{12,8},{9,1... | collective-permute-start | bytes 110600 | tf_op jit(solution)/shard_map/ppermute | solution.py:35
  15.8 9.6 %collective-permute-start.16 = (bf16[96,384]{1,0:T(8,128)(2,1)S(1)}, bf16[96,384]{1,0:T(8,128)(2,1)S(1)}, u32[]{:S(2)}, u32[]{:S(2)}) collective-permute-start(bf16[96,384]{1,0:T(8,128)(2,1)S(1)} %maximum_select_fusion.3), channel_id=1, source_target_pairs={{0,136},{8,128},{128,8},{136,0},{1,137},{9,129},{129,9},{137,1},{2... | collective-permute-start | bytes 221192 | tf_op jit(solution)/shard_map/ppermute | solution.py:35
  19.2 6.2 %collective-permute-start.15 = (bf16[96,384]{1,0:T(8,128)(2,1)S(1)}, bf16[96,384]{1,0:T(8,128)(2,1)S(1)}, u32[]{:S(2)}, u32[]{:S(2)}) collective-permute-start(bf16[96,384]{1,0:T(8,128)(2,1)S(1)} %maximum_select_fusion.3), channel_id=1, source_target_pairs={{0,128},{128,0},{1,129},{129,1},{2,130},{130,2},{3,131},{131,3},{4... | collective-permute-start | bytes 221192 | tf_op jit(solution)/shard_map/ppermute | solution.py:35
  19.5 5.9 %collective-permute-start.14 = (bf16[96,384]{1,0:T(8,128)(2,1)S(1)}, bf16[96,384]{1,0:T(8,128)(2,1)S(1)}, u32[]{:S(2)}, u32[]{:S(2)}) collective-permute-start(bf16[96,384]{1,0:T(8,128)(2,1)S(1)} %maximum_select_fusion.3), channel_id=1, source_target_pairs={{0,8},{8,0},{1,9},{9,1},{2,10},{10,2},{3,11},{11,3},{4,12},{12,4},... | collective-permute-start | bytes 221192 | tf_op jit(solution)/shard_map/ppermute | solution.py:35
  26.2 21.9 %collective-permute-start.1 = (bf16[128,3840]{1,0:T(8,128)(2,1)S(1)}, bf16[128,3840]{1,0:T(8,128)(2,1)S(1)}, u32[]{:S(2)}, u32[]{:S(2)}) collective-permute-start(bf16[128,3840]{1,0:T(8,128)(2,1)S(1)} %copy-done.13), channel_id=1, source_target_pairs={{0,4},{4,0},{1,5},{5,1},{2,6},{6,2},{3,7},{7,3},{8,12},{12,8},{9,1... | collective-permute-start | bytes 2949128 | tf_op jit(solution)/shard_map/ppermute | solution.py:35
  28.1 21.9 %collective-permute-start = (bf16[128,3840]{1,0:T(8,128)(2,1)S(1)}, bf16[128,3840]{1,0:T(8,128)(2,1)}, u32[]{:S(2)}, u32[]{:S(2)}) collective-permute-start(bf16[128,3840]{1,0:T(8,128)(2,1)S(1)} %copy-done.13), channel_id=1, source_target_pairs={{0,2},{2,0},{1,3},{3,1},{4,6},{6,4},{5,7},{7,5},{8,10},{10,8},{9,1... | collective-permute-start | bytes 2949128 | tf_op jit(solution)/shard_map/ppermute | solution.py:35
  31.4 26.5 %collective-permute-start.17 = (bf16[768,768]{1,0:T(8,128)(2,1)S(1)}, bf16[768,768]{1,0:T(8,128)(2,1)S(1)}, u32[]{:S(2)}, u32[]{:S(2)}) collective-permute-start(bf16[768,768]{1,0:T(8,128)(2,1)S(1)} %pad_maximum_fusion), channel_id=1, source_target_pairs={{0,130},{2,128},{128,2},{130,0},{1,131},{3,129},{129,3},{131,1},{4... | collective-permute-start | bytes 3538952 | tf_op jit(solution)/shard_map/ppermute | solution.py:35
  33.7 30.0 %collective-permute-start.4 = (bf16[128,3840]{1,0:T(8,128)(2,1)S(1)}, bf16[128,3840]{1,0:T(8,128)(2,1)S(1)}, u32[]{:S(2)}, u32[]{:S(2)}) collective-permute-start(bf16[128,3840]{1,0:T(8,128)(2,1)S(1)} %copy-done.11), channel_id=1, source_target_pairs={{0,1},{1,0},{2,3},{3,2},{4,5},{5,4},{6,7},{7,6},{8,9},{9,8},{10,11... | collective-permute-start | bytes 2949128 | tf_op jit(solution)/shard_map/ppermute | solution.py:35
  50.0 12.1 %collective-permute-start.5 = (bf16[128,1536]{1,0:T(8,128)(2,1)S(1)}, bf16[128,1536]{1,0:T(8,128)(2,1)S(1)}, u32[]{:S(2)}, u32[]{:S(2)}) collective-permute-start(bf16[128,1536]{1,0:T(8,128)(2,1)S(1)} %copy-done.15), channel_id=1, source_target_pairs={{0,2},{2,0},{1,3},{3,1},{4,6},{6,4},{5,7},{7,5},{8,10},{10,8},{9,1... | collective-permute-start | bytes 1179656 | tf_op jit(solution)/shard_map/ppermute | solution.py:35
  51.6 5.7 %collective-permute-start.7 = (bf16[128,768]{1,0:T(8,128)(2,1)S(1)}, bf16[128,768]{1,0:T(8,128)(2,1)S(1)}, u32[]{:S(2)}, u32[]{:S(2)}) collective-permute-start(bf16[128,768]{1,0:T(8,128)(2,1)S(1)} %copy-done.18), channel_id=1, source_target_pairs={{0,4},{4,0},{1,5},{5,1},{2,6},{6,2},{3,7},{7,3},{8,12},{12,8},{9,1... | collective-permute-start | bytes 589832 | tf_op jit(solution)/shard_map/ppermute | solution.py:35
  51.9 16.5 %collective-permute-start.10 = (bf16[64,3840]{1,0:T(8,128)(2,1)S(1)}, bf16[64,3840]{1,0:T(8,128)(2,1)}, u32[]{:S(2)}, u32[]{:S(2)}) collective-permute-start(bf16[64,3840]{1,0:T(8,128)(2,1)S(1)} %slice.19), channel_id=1, source_target_pairs={{0,2},{2,0},{1,3},{3,1},{4,6},{6,4},{5,7},{7,5},{8,10},{10,8},{9,1... | collective-permute-start | bytes 1474568 | tf_op jit(solution)/shard_map/ppermute | solution.py:35
  57.3 6.9 %collective-permute-start.8 = (bf16[128,768]{1,0:T(8,128)(2,1)S(1)}, bf16[128,768]{1,0:T(8,128)(2,1)S(1)}, u32[]{:S(2)}, u32[]{:S(2)}) collective-permute-start(bf16[128,768]{1,0:T(8,128)(2,1)S(1)} %collective-permute-done.7.refs_13_), channel_id=1, source_target_pairs={{0,1},{1,0},{2,3},{3,2},{4,5},{5,4},{6,7},{7,6},{8,9},{9,8},{10,11... | collective-permute-start | bytes 589832 | tf_op jit(solution)/shard_map/ppermute | solution.py:35
  62.3 18.1 %collective-permute-start.18 = (bf16[768,768]{1,0:T(8,128)(2,1)S(1)}, bf16[768,768]{1,0:T(8,128)(2,1)}, u32[]{:S(2)}, u32[]{:S(2)}) collective-permute-start(bf16[768,768]{1,0:T(8,128)(2,1)S(1)} %pad_maximum_fusion.1), channel_id=1, source_target_pairs={{0,1},{1,0},{2,3},{3,2},{4,5},{5,4},{6,7},{7,6},{8,9},{9,8},{10,11... | collective-permute-start | bytes 3538952 | tf_op jit(solution)/shard_map/ppermute | solution.py:35
  63.5 13.8 %collective-permute-start.9 = (bf16[64,3840]{1,0:T(8,128)(2,1)S(1)}, bf16[64,3840]{1,0:T(8,128)(2,1)}, u32[]{:S(2)}, u32[]{:S(2)}) collective-permute-start(bf16[64,3840]{1,0:T(8,128)(2,1)S(1)} %slice.18), channel_id=1, source_target_pairs={{0,4},{4,0},{1,5},{5,1},{2,6},{6,2},{3,7},{7,3},{8,12},{12,8},{9,1... | collective-permute-start | bytes 1474568 | tf_op jit(solution)/shard_map/ppermute | solution.py:35
  63.8 16.6 %collective-permute-start.2 = (bf16[128,3840]{1,0:T(8,128)(2,1)}, bf16[128,3840]{1,0:T(8,128)(2,1)S(1)}, u32[]{:S(2)}, u32[]{:S(2)}) collective-permute-start(bf16[128,3840]{1,0:T(8,128)(2,1)} %collective-permute-done.refs_6_), channel_id=1, source_target_pairs={{0,1},{1,0},{2,3},{3,2},{4,5},{5,4},{6,7},{7,6},{8,9},{9,8},{10,11... | collective-permute-start | bytes 2949128 | tf_op jit(solution)/shard_map/ppermute | solution.py:35
  64.2 16.2 %collective-permute-start.3 = (bf16[128,3840]{1,0:T(8,128)(2,1)S(1)}, bf16[128,3840]{1,0:T(8,128)(2,1)}, u32[]{:S(2)}, u32[]{:S(2)}) collective-permute-start(bf16[128,3840]{1,0:T(8,128)(2,1)S(1)} %collective-permute-done.1.refs_8_), channel_id=1, source_target_pairs={{0,1},{1,0},{2,3},{3,2},{4,5},{5,4},{6,7},{7,6},{8,9},{9,8},{10,11... | collective-permute-start | bytes 2949128 | tf_op jit(solution)/shard_map/ppermute | solution.py:35
  68.4 8.9 %collective-permute-start.6 = (bf16[128,1536]{1,0:T(8,128)(2,1)S(1)}, bf16[128,1536]{1,0:T(8,128)(2,1)S(1)}, u32[]{:S(2)}, u32[]{:S(2)}) collective-permute-start(bf16[128,1536]{1,0:T(8,128)(2,1)S(1)} %collective-permute-done.5.refs_11_), channel_id=1, source_target_pairs={{0,1},{1,0},{2,3},{3,2},{4,5},{5,4},{6,7},{7,6},{8,9},{9,8},{10,11... | collective-permute-start | bytes 1179656 | tf_op jit(solution)/shard_map/ppermute | solution.py:35
  78.0 2.3 %collective-permute-start.11 = (bf16[64,3840]{1,0:T(8,128)(2,1)}, bf16[64,3840]{1,0:T(8,128)(2,1)}, u32[]{:S(2)}, u32[]{:S(2)}) collective-permute-start(bf16[64,3840]{1,0:T(8,128)(2,1)} %collective-permute-done.9.refs_15_), channel_id=1, source_target_pairs={{0,1},{1,0},{2,3},{3,2},{4,5},{5,4},{6,7},{7,6},{8,9},{9,8},{10,11... | collective-permute-start | bytes 1474568 | tf_op jit(solution)/shard_map/ppermute | solution.py:35
  99.1 4.5 %collective-permute-start.22 = (f32[8,128]{1,0:T(8,128)S(1)}, f32[8,128]{1,0:T(8,128)S(1)}, u32[]{:S(2)}, u32[]{:S(2)}) collective-permute-start(f32[8,128]{1,0:T(8,128)S(1)} %add.126.refs_0_), channel_id=1, source_target_pairs={{0,6},{2,4},{4,2},{6,0},{1,7},{3,5},{5,3},{7,1},{8,14},{10,12},{12... | collective-permute-start | bytes 12296 | tf_op jit(solution)/shard_map/ppermute | solution.py:35
  100.4 3.6 %collective-permute-start.21 = (f32[8,128]{1,0:T(8,128)S(1)}, f32[8,128]{1,0:T(8,128)S(1)}, u32[]{:S(2)}, u32[]{:S(2)}) collective-permute-start(f32[8,128]{1,0:T(8,128)S(1)} %add.126.refs_0_), channel_id=1, source_target_pairs={{0,2},{2,0},{1,3},{3,1},{4,6},{6,4},{5,7},{7,5},{8,10},{10,8},{9,1... | collective-permute-start | bytes 12296 | tf_op jit(solution)/shard_map/ppermute | solution.py:35
  100.9 3.6 %collective-permute-start.20 = (f32[8,128]{1,0:T(8,128)S(1)}, f32[8,128]{1,0:T(8,128)S(1)}, u32[]{:S(2)}, u32[]{:S(2)}) collective-permute-start(f32[8,128]{1,0:T(8,128)S(1)} %add.126.refs_0_), channel_id=1, source_target_pairs={{0,4},{4,0},{1,5},{5,1},{2,6},{6,2},{3,7},{7,3},{8,12},{12,8},{9,1... | collective-permute-start | bytes 12296 | tf_op jit(solution)/shard_map/ppermute | solution.py:35
  107.9 27.4 %collective-permute-start.28 = (bf16[784,384]{1,0:T(8,128)(2,1)}, bf16[784,384]{1,0:T(8,128)(2,1)S(1)}, u32[]{:S(2)}, u32[]{:S(2)}) collective-permute-start(bf16[784,384]{1,0:T(8,128)(2,1)} %get-tuple-element.60), channel_id=1, source_target_pairs={{0,136},{8,128},{128,8},{136,0},{1,137},{9,129},{129,9},{137,1},{2... | collective-permute-start | bytes 1806344 | tf_op jit(solution)/shard_map/ppermute | solution.py:35
  111.5 27.9 %collective-permute-start.27 = (bf16[784,384]{1,0:T(8,128)(2,1)}, bf16[784,384]{1,0:T(8,128)(2,1)S(1)}, u32[]{:S(2)}, u32[]{:S(2)}) collective-permute-start(bf16[784,384]{1,0:T(8,128)(2,1)} %get-tuple-element.61), channel_id=1, source_target_pairs={{0,128},{128,0},{1,129},{129,1},{2,130},{130,2},{3,131},{131,3},{4... | collective-permute-start | bytes 1806344 | tf_op jit(solution)/shard_map/ppermute | solution.py:35
  112.0 27.6 %collective-permute-start.26 = (bf16[784,384]{1,0:T(8,128)(2,1)}, bf16[784,384]{1,0:T(8,128)(2,1)S(1)}, u32[]{:S(2)}, u32[]{:S(2)}) collective-permute-start(bf16[784,384]{1,0:T(8,128)(2,1)} %get-tuple-element.62), channel_id=1, source_target_pairs={{0,8},{8,0},{1,9},{9,1},{2,10},{10,2},{3,11},{11,3},{4,12},{12,4},... | collective-permute-start | bytes 1806344 | tf_op jit(solution)/shard_map/ppermute | solution.py:35
  116.4 3.7 %collective-permute-start.23 = (f32[]{:T(128)}, f32[]{:T(128)}, u32[]{:S(2)}, u32[]{:S(2)}) collective-permute-start(f32[]{:T(128)} %select_n.85), channel_id=1, source_target_pairs={{0,16},{16,0},{32,48},{48,32},{64,80},{80,64},{96,112},{112,96},{1... | collective-permute-start | bytes 20 | tf_op jit(solution)/shard_map/ppermute | solution.py:356
  120.7 5.0 %collective-permute-start.24 = (f32[]{:T(128)}, f32[]{:T(128)}, u32[]{:S(2)}, u32[]{:S(2)}) collective-permute-start(f32[]{:T(128)} %add.128), channel_id=1, source_target_pairs={{0,32},{16,48},{32,0},{48,16},{64,96},{80,112},{96,64},{112,80},{1... | collective-permute-start | bytes 20 | tf_op jit(solution)/shard_map/ppermute | solution.py:356
  126.2 8.6 %collective-permute-start.25 = (f32[]{:T(128)}, f32[]{:T(128)}, u32[]{:S(2)}, u32[]{:S(2)}) collective-permute-start(f32[]{:T(128)} %add.129), channel_id=1, source_target_pairs={{0,64},{16,80},{32,96},{48,112},{64,0},{80,16},{96,32},{112,48},{1... | collective-permute-start | bytes 20 | tf_op jit(solution)/shard_map/ppermute | solution.py:356
  143.2 28.1 %all-to-all-start = ((bf16[16,48,384]{2,1,0:T(8,128)(2,1)}), bf16[16,48,384]{2,1,0:T(8,128)(2,1)S(1)}, u32[]{:S(2)}, u32[]{:S(2)}) async-start(bf16[16,48,384]{2,1,0:T(8,128)(2,1)} %bitcast.24), calls=%async_computation | async-start | bytes 1179648 | tf_op jit(solution)/shard_map/all_to_all | solution.py:363
  153.4 12.5 %collective-permute-start.31 = (f32[]{:T(128)}, f32[]{:T(128)}, u32[]{:S(2)}, u32[]{:S(2)}) collective-permute-start(f32[]{:T(128)} %add.130), channel_id=1, source_target_pairs={{0,136},{8,128},{128,8},{136,0},{1,137},{9,129},{129,9},{137,1},{2... | collective-permute-start | bytes 20 | tf_op jit(solution)/shard_map/ppermute | solution.py:35
  157.7 8.1 %collective-permute-start.30 = (f32[]{:T(128)}, f32[]{:T(128)}, u32[]{:S(2)}, u32[]{:S(2)}) collective-permute-start(f32[]{:T(128)} %add.130), channel_id=1, source_target_pairs={{0,128},{128,0},{1,129},{129,1},{2,130},{130,2},{3,131},{131,3},{4... | collective-permute-start | bytes 20 | tf_op jit(solution)/shard_map/ppermute | solution.py:35
  160.0 5.2 %collective-permute-start.29 = (f32[]{:T(128)}, f32[]{:T(128)}, u32[]{:S(2)}, u32[]{:S(2)}) collective-permute-start(f32[]{:T(128)} %add.130), channel_id=1, source_target_pairs={{0,8},{8,0},{1,9},{9,1},{2,10},{10,2},{3,11},{11,3},{4,12},{12,4},... | collective-permute-start | bytes 20 | tf_op jit(solution)/shard_map/ppermute | solution.py:35
  (23 other events, 196.9 us)
Sparse Core Ops, SparseCore 0:
  26.3 43.5 all-gather.1

commit v4 on v3

--- a/solution.py
+++ b/solution.py
@@ -315,20 +315,20 @@
 
     send, send_c, weight_in, _ = lax.optimization_barrier((send, send_c, reference_weight, same_z))
     rows_y, rows_x, got_c = flip(send, "yl"), flip(send, "xl"), flip(send_c, "c")
-    send_y, send_x, rows_y, rows_x = lax.optimization_barrier((send_y, send_x, rows_y, rows_x))
-    got_y, got_x = flip(send_y, "yl"), flip(send_x, "xl")
 
     ref_y = flip(
         jnp.concatenate([columns(weight_in, 0, 1, 0), columns(weight_in, 0, 1, 1)], 1), "yh", "yl"
     )
-    ref_y = after(ref_y, got_y)
-    ref_c = flip(jnp.concatenate([columns(weight_in, 0, 0, 1), ref_y[:, half:]], 1), "c")
+    send_y, send_x = after(send_y, rows_y, rows_x), after(send_x, rows_y, rows_x, ref_y)
+    got_y, got_x = flip(send_y, "yl"), flip(send_x, "xl")
 
     n_z = SIZES[1]
     per_z = lax.all_gather(same_z.reshape(-1, half), "z").reshape(n_z, 2, -1, half)
 
     h = tok // 2
     diag = [flip(rows_y[:h], "xl"), flip(rows_x[h:], "yl")]
+    ref_y = after(ref_y, *diag)
+    ref_c = flip(jnp.concatenate([columns(weight_in, 0, 0, 1), ref_y[:, half:]], 1), "c")
     diag_c = [flip(part, "c") for part in diag]
     rows_yc, rows_xc = flip(rows_y, "c"), flip(rows_x, "c")
     got_yc, got_xc = flip(got_y, "c"), flip(got_x, "c")

time: 181 us -> 177 us (0.978)
  waiting for transfers between devices: 56.4 us -> 49.7 us
  starting transfers between devices: 65.8 us -> 68 us
    ppermute x29, waiting for transfers between devices: 51.1 us -> 44.6 us  [flip(): return lax.ppermute(x, axes, [(i, last - i) for i in range(last + 1)])]
    ppermute x29, starting transfers between devices: 39.4 us -> 41.7 us  [flip(): return lax.ppermute(x, axes, [(i, last - i) for i in range(last + 1)])]
  transfers between devices with their start and end apart: 34 -> 34, of which waited for: 21 -> 20; matrix products, arithmetic and copies ran while one was open for 3% -> 3% of each run, Pallas kernels for 3% -> 3%
where the time goes in v4:
time: 177 us; the launch traced here: 176 us
  starting transfers between devices  68 us (38%)
  waiting for transfers between devices  49.7 us (28%)
  Pallas kernels  23.5 us (13%)
  between operations  19.7 us (11%)
  local copies, waits for them, and re-layouts  11.6 us (7%)
  other arithmetic  3.54 us (2%)
    ppermute x29, waiting for transfers between devices, flip(): return lax.ppermute(x, axes, [(i, last - i) for i in range(last + 1)])  44.6 us
    ppermute x29, starting transfers between devices, flip(): return lax.ppermute(x, axes, [(i, last - i) for i in range(last + 1)])  41.7 us
    ppermute x3, starting transfers between devices, body(): loss = loss + lax.ppermute(loss, 'z', [(i, i ^ step) for i in range(n_z)])  16.2 us
    pallas_call x1, Pallas kernels, project(): pl.pallas_call(lambda *refs: project_kernel(half, *refs), in_specs=[small...  15.7 us
    all_to_all x1, starting transfers between devices, body(): lax.all_to_all(summed.reshape(-1, rows, half), ('z', 'xl'), split_axis=0,...  10.1 us
    unnamed x42, local copies, waits for them, and re-layouts  5.06 us
    pallas_call x1, Pallas kernels, pack(): pl.pallas_call(lambda *refs: pack_kernel(half, *refs), grid=(tok // rows,...  4.62 us
    all_to_all x1, waiting for transfers between devices, body(): lax.all_to_all(summed.reshape(-1, rows, half), ('z', 'xl'), split_axis=0,...  3.99 us
  transfers between devices with their start and end apart: 34, of which 20 were waited for; matrix products, arithmetic and copies ran while one was open for 3% of the time, Pallas kernels for 3%

profile of v4, /device:TPU:2, one launch (start us, length us, event | category | flops | bytes accessed | tf_op | source)
XLA Modules:
  0.0 176.1 jit_solution(17665827806974186102)
XLA Ops:
  8.2 2.4 %collective-permute-start.14 = (bf16[48,384]{1,0:T(8,128)(2,1)S(1)}, bf16[48,384]{1,0:T(8,128)(2,1)S(1)}, u32[]{:S(2)}, u32[]{:S(2)}) collective-permute-start(bf16[48,384]{1,0:T(8,128)(2,1)S(1)} %get-tuple-element.55), channel_id=1, source_target_pairs={{0,4},{4,0},{1,5},{5,1},{2,6},{6,2},{3,7},{7,3},{8,12},{12,8},{9,1... | collective-permute-start | bytes 110600 | tf_op jit(solution)/shard_map/ppermute | solution.py:35
  11.1 4.6 %pack.1 = (bf16[128,3072]{1,0:T(8,128)(2,1)}, bf16[128,3840]{1,0:T(8,128)(2,1)}, bf16[128,1536]{1,0:T(8,128)(2,1)}, bf16[128,768]{1,0:T(8,128)(2,1)}, bf16[128,3840]{1,0:T(8,128)(2,1)}) custom-call(s32[9]{0:T(128)} %stack.70.refs_0_, s32[32]{0:T(128)} %refs_1_.3, bf16[128,3072]{1,0:T(8,128)(2,1)} %refs_3_.3, bf16[128,3072]{1,0:T(8,128)(2,1)} %refs_4_.1, ...), custom_call_target="tpu_custom_call" | custom-call | flops 7864320 | bytes 5898240 | tf_op jit(solution)/shard_map/pack/pallas_call | solution.py:80
  15.8 3.4 %collective-permute-start.17 = (bf16[96,384]{1,0:T(8,128)(2,1)S(1)}, bf16[96,384]{1,0:T(8,128)(2,1)S(1)}, u32[]{:S(2)}, u32[]{:S(2)}) collective-permute-start(bf16[96,384]{1,0:T(8,128)(2,1)S(1)} %maximum_select_fusion.3), channel_id=1, source_target_pairs={{0,136},{8,128},{128,8},{136,0},{1,137},{9,129},{129,9},{137,1},{2... | collective-permute-start | bytes 221192 | tf_op jit(solution)/shard_map/ppermute | solution.py:35
  19.5 2.8 %collective-permute-start.15 = (bf16[96,384]{1,0:T(8,128)(2,1)S(1)}, bf16[96,384]{1,0:T(8,128)(2,1)S(1)}, u32[]{:S(2)}, u32[]{:S(2)}) collective-permute-start(bf16[96,384]{1,0:T(8,128)(2,1)S(1)} %maximum_select_fusion.3), channel_id=1, source_target_pairs={{0,8},{8,0},{1,9},{9,1},{2,10},{10,2},{3,11},{11,3},{4,12},{12,4},... | collective-permute-start | bytes 221192 | tf_op jit(solution)/shard_map/ppermute | solution.py:35
  22.4 3.0 %collective-permute-done.15 = bf16[96,384]{1,0:T(8,128)(2,1)S(1)} collective-permute-done((bf16[96,384]{1,0:T(8,128)(2,1)S(1)}, bf16[96,384]{1,0:T(8,128)(2,1)S(1)}, u32[]{:S(2)}, u32[]{:S(2)}) %collective-permute-start.15) | collective-permute-done | bytes 73760 | tf_op jit(solution)/shard_map/ppermute | solution.py:35
  26.2 1.9 %collective-permute-start.2 = (bf16[128,3840]{1,0:T(8,128)(2,1)S(1)}, bf16[128,3840]{1,0:T(8,128)(2,1)S(1)}, u32[]{:S(2)}, u32[]{:S(2)}) collective-permute-start(bf16[128,3840]{1,0:T(8,128)(2,1)S(1)} %copy-done.13), channel_id=1, source_target_pairs={{0,4},{4,0},{1,5},{5,1},{2,6},{6,2},{3,7},{7,3},{8,12},{12,8},{9,1... | collective-permute-start | bytes 2949128 | tf_op jit(solution)/shard_map/ppermute | solution.py:35
  28.1 1.6 collective-permute-start
  29.7 1.6 constant_dynamic-slice_fusion
  31.4 2.3 %collective-permute-start.7 = (bf16[768,768]{1,0:T(8,128)(2,1)S(1)}, bf16[768,768]{1,0:T(8,128)(2,1)S(1)}, u32[]{:S(2)}, u32[]{:S(2)}) collective-permute-start(bf16[768,768]{1,0:T(8,128)(2,1)S(1)} %pad_maximum_fusion), channel_id=1, source_target_pairs={{0,130},{2,128},{128,2},{130,0},{1,131},{3,129},{129,3},{131,1},{4... | collective-permute-start | bytes 3538952 | tf_op jit(solution)/shard_map/ppermute | solution.py:35
  33.7 14.4 %collective-permute-done.2.refs_8_ = bf16[128,3840]{1,0:T(8,128)(2,1)S(1)} collective-permute-done((bf16[128,3840]{1,0:T(8,128)(2,1)S(1)}, bf16[128,3840]{1,0:T(8,128)(2,1)S(1)}, u32[]{:S(2)}, u32[]{:S(2)}) %collective-permute-start.2) | collective-permute-done | bytes 983072 | tf_op jit(solution)/shard_map/ppermute | solution.py:35
  48.2 1.7 collective-permute-start.11
  53.4 4.5 %collective-permute-done.7.refs_21_ = bf16[768,768]{1,0:T(8,128)(2,1)S(1)} collective-permute-done((bf16[768,768]{1,0:T(8,128)(2,1)S(1)}, bf16[768,768]{1,0:T(8,128)(2,1)S(1)}, u32[]{:S(2)}, u32[]{:S(2)}) %collective-permute-start.7) | collective-permute-done | bytes 1179680 | tf_op jit(solution)/shard_map/ppermute | solution.py:35
  57.9 4.6 %collective-permute-done.11.refs_16_ = bf16[64,3840]{1,0:T(8,128)(2,1)} collective-permute-done((bf16[64,3840]{1,0:T(8,128)(2,1)S(1)}, bf16[64,3840]{1,0:T(8,128)(2,1)}, u32[]{:S(2)}, u32[]{:S(2)}) %collective-permute-start.11) | collective-permute-done | bytes 491552 | tf_op jit(solution)/shard_map/ppermute | solution.py:35
  64.5 1.5 collective-permute-start.8
  66.0 2.3 %collective-permute-done.5.refs_11_ = bf16[128,1536]{1,0:T(8,128)(2,1)S(1)} collective-permute-done((bf16[128,1536]{1,0:T(8,128)(2,1)S(1)}, bf16[128,1536]{1,0:T(8,128)(2,1)S(1)}, u32[]{:S(2)}, u32[]{:S(2)}) %collective-permute-start.5) | collective-permute-done | bytes 393248 | tf_op jit(solution)/shard_map/ppermute | solution.py:35
  69.1 2.7 %collective-permute-done.8.refs_13_ = bf16[128,768]{1,0:T(8,128)(2,1)S(1)} collective-permute-done((bf16[128,768]{1,0:T(8,128)(2,1)S(1)}, bf16[128,768]{1,0:T(8,128)(2,1)S(1)}, u32[]{:S(2)}, u32[]{:S(2)}) %collective-permute-start.8) | collective-permute-done | bytes 196640 | tf_op jit(solution)/shard_map/ppermute | solution.py:35
  76.3 15.7 %project.1 = (f32[8,128]{1,0:T(8,128)}, bf16[784,384]{1,0:T(8,128)(2,1)}, bf16[784,384]{1,0:T(8,128)(2,1)}, bf16[784,384]{1,0:T(8,128)(2,1)}, bf16[784,384]{1,0:T(8,128)(2,1)}) custom-call(s32[7]{0:T(128)} %stack.62.refs_0_, s32[32]{0:T(128)} %refs_1_.3, s32[32]{0:T(128)} %refs_2_.3, bf16[128,3072]{1,0:T(8,128)(2,1)} %refs_3_.3, bf16[128,3072]{1,0:T(8,128)(2,1)} %refs_4_.1, ...), custom_call_target="tpu_custom_call" | custom-call | flops 7247757312 | bytes 16777216 | tf_op jit(solution)/shard_map/project/pallas_call | solution.py:216
  94.2 2.5 %collective-permute-start.22 = (f32[8,128]{1,0:T(8,128)S(1)}, f32[8,128]{1,0:T(8,128)S(1)}, u32[]{:S(2)}, u32[]{:S(2)}) collective-permute-start(f32[8,128]{1,0:T(8,128)S(1)} %add.126.refs_0_), channel_id=1, source_target_pairs={{0,6},{2,4},{4,2},{6,0},{1,7},{3,5},{5,3},{7,1},{8,14},{10,12},{12... | collective-permute-start | bytes 12296 | tf_op jit(solution)/shard_map/ppermute | solution.py:35
  98.7 1.6 collective-permute-done.21.refs_2_
  104.2 3.0 %collective-permute-start.28 = (bf16[784,384]{1,0:T(8,128)(2,1)}, bf16[784,384]{1,0:T(8,128)(2,1)S(1)}, u32[]{:S(2)}, u32[]{:S(2)}) collective-permute-start(bf16[784,384]{1,0:T(8,128)(2,1)} %get-tuple-element.56), channel_id=1, source_target_pairs={{0,136},{8,128},{128,8},{136,0},{1,137},{9,129},{129,9},{137,1},{2... | collective-permute-start | bytes 1806344 | tf_op jit(solution)/shard_map/ppermute | solution.py:35
  108.3 2.3 %collective-permute-start.26 = (bf16[784,384]{1,0:T(8,128)(2,1)}, bf16[784,384]{1,0:T(8,128)(2,1)S(1)}, u32[]{:S(2)}, u32[]{:S(2)}) collective-permute-start(bf16[784,384]{1,0:T(8,128)(2,1)} %get-tuple-element.58), channel_id=1, source_target_pairs={{0,8},{8,0},{1,9},{9,1},{2,10},{10,2},{3,11},{11,3},{4,12},{12,4},... | collective-permute-start | bytes 1806344 | tf_op jit(solution)/shard_map/ppermute | solution.py:35
  112.6 3.3 %collective-permute-start.23 = (f32[]{:T(128)}, f32[]{:T(128)}, u32[]{:S(2)}, u32[]{:S(2)}) collective-permute-start(f32[]{:T(128)} %select_n.85), channel_id=1, source_target_pairs={{0,16},{16,0},{32,48},{48,32},{64,80},{80,64},{96,112},{112,96},{1... | collective-permute-start | bytes 20 | tf_op jit(solution)/shard_map/ppermute | solution.py:356
  116.9 4.7 %collective-permute-start.24 = (f32[]{:T(128)}, f32[]{:T(128)}, u32[]{:S(2)}, u32[]{:S(2)}) collective-permute-start(f32[]{:T(128)} %add.128), channel_id=1, source_target_pairs={{0,32},{16,48},{32,0},{48,16},{64,96},{80,112},{96,64},{112,80},{1... | collective-permute-start | bytes 20 | tf_op jit(solution)/shard_map/ppermute | solution.py:356
  122.4 8.2 %collective-permute-start.25 = (f32[]{:T(128)}, f32[]{:T(128)}, u32[]{:S(2)}, u32[]{:S(2)}) collective-permute-start(f32[]{:T(128)} %add.129), channel_id=1, source_target_pairs={{0,64},{16,80},{32,96},{48,112},{64,0},{80,16},{96,32},{112,48},{1... | collective-permute-start | bytes 20 | tf_op jit(solution)/shard_map/ppermute | solution.py:356
  131.6 4.0 %collective-permute-done.27.refs_3_ = bf16[784,384]{1,0:T(8,128)(2,1)S(1)} collective-permute-done((bf16[784,384]{1,0:T(8,128)(2,1)}, bf16[784,384]{1,0:T(8,128)(2,1)S(1)}, u32[]{:S(2)}, u32[]{:S(2)}) %collective-permute-start.27) | collective-permute-done | bytes 602144 | tf_op jit(solution)/shard_map/ppermute | solution.py:35
  137.3 1.9 %combine.1 = bf16[768,384]{1,0:T(8,128)(2,1)} custom-call(f32[8,128]{1,0:T(8,128)S(1)} %copy-done.1, bf16[784,384]{1,0:T(8,128)(2,1)S(1)} %copy-done, bf16[784,384]{1,0:T(8,128)(2,1)S(1)} %collective-permute-done.26.refs_2_, bf16[784,384]{1,0:T(8,128)(2,1)S(1)} %collective-permute-done.27.refs_3_, bf16[784,384]{1,0:T(8,128)(2,1)S(1)} %collective-permute-done.28.refs_4_), custom_call_target="tpu_custom_call" | custom-call | tf_op jit(solution)/shard_map/combine/pallas_call | solution.py:277
  139.2 10.1 %all-to-all-start = ((bf16[16,48,384]{2,1,0:T(8,128)(2,1)}), bf16[16,48,384]{2,1,0:T(8,128)(2,1)S(1)}, u32[]{:S(2)}, u32[]{:S(2)}) async-start(bf16[16,48,384]{2,1,0:T(8,128)(2,1)} %bitcast.24), calls=%async_computation | async-start | bytes 1179648 | tf_op jit(solution)/shard_map/all_to_all | solution.py:363
  149.3 4.5 %collective-permute-start.31 = (f32[]{:T(128)}, f32[]{:T(128)}, u32[]{:S(2)}, u32[]{:S(2)}) collective-permute-start(f32[]{:T(128)} %add.130), channel_id=1, source_target_pairs={{0,136},{8,128},{128,8},{136,0},{1,137},{9,129},{129,9},{137,1},{2... | collective-permute-start | bytes 20 | tf_op jit(solution)/shard_map/ppermute | solution.py:35
  153.8 2.4 %collective-permute-start.30 = (f32[]{:T(128)}, f32[]{:T(128)}, u32[]{:S(2)}, u32[]{:S(2)}) collective-permute-start(f32[]{:T(128)} %add.130), channel_id=1, source_target_pairs={{0,128},{128,0},{1,129},{129,1},{2,130},{130,2},{3,131},{131,3},{4... | collective-permute-start | bytes 20 | tf_op jit(solution)/shard_map/ppermute | solution.py:35
  156.2 3.6 %collective-permute-start.29 = (f32[]{:T(128)}, f32[]{:T(128)}, u32[]{:S(2)}, u32[]{:S(2)}) collective-permute-start(f32[]{:T(128)} %add.130), channel_id=1, source_target_pairs={{0,8},{8,0},{1,9},{9,1},{2,10},{10,2},{3,11},{11,3},{4,12},{12,4},... | collective-permute-start | bytes 20 | tf_op jit(solution)/shard_map/ppermute | solution.py:35
  159.8 1.5 collective-permute-done.29
  163.2 4.0 %all-to-all-done = bf16[16,48,384]{2,1,0:T(8,128)(2,1)S(1)} async-done(((bf16[16,48,384]{2,1,0:T(8,128)(2,1)}), bf16[16,48,384]{2,1,0:T(8,128)(2,1)S(1)}, u32[]{:S(2)}, u32[]{:S(2)}) %all-to-all-start) | async-done | bytes 589856 | tf_op jit(solution)/shard_map/all_to_all | solution.py:363
  (104 shorter events, 27.9 us)
Async XLA Ops:
  7.2 69.1 %all-gather.2.cloned.1.call-start = ((), (), s32[]{:S(2)}) async-start(), calls=%async_computation.1 | async-start | bytes 2654208 | tf_op jit(solution)/shard_map/all_gather | solution.py:326
  8.2 7.6 %collective-permute-start.14 = (bf16[48,384]{1,0:T(8,128)(2,1)S(1)}, bf16[48,384]{1,0:T(8,128)(2,1)S(1)}, u32[]{:S(2)}, u32[]{:S(2)}) collective-permute-start(bf16[48,384]{1,0:T(8,128)(2,1)S(1)} %get-tuple-element.55), channel_id=1, source_target_pairs={{0,4},{4,0},{1,5},{5,1},{2,6},{6,2},{3,7},{7,3},{8,12},{12,8},{9,1... | collective-permute-start | bytes 110600 | tf_op jit(solution)/shard_map/ppermute | solution.py:35
  15.8 9.6 %collective-permute-start.17 = (bf16[96,384]{1,0:T(8,128)(2,1)S(1)}, bf16[96,384]{1,0:T(8,128)(2,1)S(1)}, u32[]{:S(2)}, u32[]{:S(2)}) collective-permute-start(bf16[96,384]{1,0:T(8,128)(2,1)S(1)} %maximum_select_fusion.3), channel_id=1, source_target_pairs={{0,136},{8,128},{128,8},{136,0},{1,137},{9,129},{129,9},{137,1},{2... | collective-permute-start | bytes 221192 | tf_op jit(solution)/shard_map/ppermute | solution.py:35
  19.2 6.2 %collective-permute-start.16 = (bf16[96,384]{1,0:T(8,128)(2,1)S(1)}, bf16[96,384]{1,0:T(8,128)(2,1)S(1)}, u32[]{:S(2)}, u32[]{:S(2)}) collective-permute-start(bf16[96,384]{1,0:T(8,128)(2,1)S(1)} %maximum_select_fusion.3), channel_id=1, source_target_pairs={{0,128},{128,0},{1,129},{129,1},{2,130},{130,2},{3,131},{131,3},{4... | collective-permute-start | bytes 221192 | tf_op jit(solution)/shard_map/ppermute | solution.py:35
  19.5 5.9 %collective-permute-start.15 = (bf16[96,384]{1,0:T(8,128)(2,1)S(1)}, bf16[96,384]{1,0:T(8,128)(2,1)S(1)}, u32[]{:S(2)}, u32[]{:S(2)}) collective-permute-start(bf16[96,384]{1,0:T(8,128)(2,1)S(1)} %maximum_select_fusion.3), channel_id=1, source_target_pairs={{0,8},{8,0},{1,9},{9,1},{2,10},{10,2},{3,11},{11,3},{4,12},{12,4},... | collective-permute-start | bytes 221192 | tf_op jit(solution)/shard_map/ppermute | solution.py:35
  26.2 21.9 %collective-permute-start.2 = (bf16[128,3840]{1,0:T(8,128)(2,1)S(1)}, bf16[128,3840]{1,0:T(8,128)(2,1)S(1)}, u32[]{:S(2)}, u32[]{:S(2)}) collective-permute-start(bf16[128,3840]{1,0:T(8,128)(2,1)S(1)} %copy-done.13), channel_id=1, source_target_pairs={{0,4},{4,0},{1,5},{5,1},{2,6},{6,2},{3,7},{7,3},{8,12},{12,8},{9,1... | collective-permute-start | bytes 2949128 | tf_op jit(solution)/shard_map/ppermute | solution.py:35
  28.1 22.4 %collective-permute-start = (bf16[128,3840]{1,0:T(8,128)(2,1)S(1)}, bf16[128,3840]{1,0:T(8,128)(2,1)}, u32[]{:S(2)}, u32[]{:S(2)}) collective-permute-start(bf16[128,3840]{1,0:T(8,128)(2,1)S(1)} %copy-done.13), channel_id=1, source_target_pairs={{0,2},{2,0},{1,3},{3,1},{4,6},{6,4},{5,7},{7,5},{8,10},{10,8},{9,1... | collective-permute-start | bytes 2949128 | tf_op jit(solution)/shard_map/ppermute | solution.py:35
  31.4 26.5 %collective-permute-start.7 = (bf16[768,768]{1,0:T(8,128)(2,1)S(1)}, bf16[768,768]{1,0:T(8,128)(2,1)S(1)}, u32[]{:S(2)}, u32[]{:S(2)}) collective-permute-start(bf16[768,768]{1,0:T(8,128)(2,1)S(1)} %pad_maximum_fusion), channel_id=1, source_target_pairs={{0,130},{2,128},{128,2},{130,0},{1,131},{3,129},{129,3},{131,1},{4... | collective-permute-start | bytes 3538952 | tf_op jit(solution)/shard_map/ppermute | solution.py:35
  33.7 29.7 %collective-permute-start.4 = (bf16[128,3840]{1,0:T(8,128)(2,1)S(1)}, bf16[128,3840]{1,0:T(8,128)(2,1)S(1)}, u32[]{:S(2)}, u32[]{:S(2)}) collective-permute-start(bf16[128,3840]{1,0:T(8,128)(2,1)S(1)} %copy-done.11), channel_id=1, source_target_pairs={{0,1},{1,0},{2,3},{3,2},{4,5},{5,4},{6,7},{7,6},{8,9},{9,8},{10,11... | collective-permute-start | bytes 2949128 | tf_op jit(solution)/shard_map/ppermute | solution.py:35
  48.2 14.4 %collective-permute-start.11 = (bf16[64,3840]{1,0:T(8,128)(2,1)S(1)}, bf16[64,3840]{1,0:T(8,128)(2,1)}, u32[]{:S(2)}, u32[]{:S(2)}) collective-permute-start(bf16[64,3840]{1,0:T(8,128)(2,1)S(1)} %slice.25), channel_id=1, source_target_pairs={{0,2},{2,0},{1,3},{3,1},{4,6},{6,4},{5,7},{7,5},{8,10},{10,8},{9,1... | collective-permute-start | bytes 1474568 | tf_op jit(solution)/shard_map/ppermute | solution.py:35
  51.6 10.9 %collective-permute-start.10 = (bf16[64,3840]{1,0:T(8,128)(2,1)S(1)}, bf16[64,3840]{1,0:T(8,128)(2,1)}, u32[]{:S(2)}, u32[]{:S(2)}) collective-permute-start(bf16[64,3840]{1,0:T(8,128)(2,1)S(1)} %slice.24), channel_id=1, source_target_pairs={{0,4},{4,0},{1,5},{5,1},{2,6},{6,2},{3,7},{7,3},{8,12},{12,8},{9,1... | collective-permute-start | bytes 1474568 | tf_op jit(solution)/shard_map/ppermute | solution.py:35
  52.5 15.8 %collective-permute-start.5 = (bf16[128,1536]{1,0:T(8,128)(2,1)S(1)}, bf16[128,1536]{1,0:T(8,128)(2,1)S(1)}, u32[]{:S(2)}, u32[]{:S(2)}) collective-permute-start(bf16[128,1536]{1,0:T(8,128)(2,1)S(1)} %copy-done.15), channel_id=1, source_target_pairs={{0,2},{2,0},{1,3},{3,1},{4,6},{6,4},{5,7},{7,5},{8,10},{10,8},{9,1... | collective-permute-start | bytes 1179656 | tf_op jit(solution)/shard_map/ppermute | solution.py:35
  62.7 13.5 %collective-permute-start.18 = (bf16[768,768]{1,0:T(8,128)(2,1)S(1)}, bf16[768,768]{1,0:T(8,128)(2,1)}, u32[]{:S(2)}, u32[]{:S(2)}) collective-permute-start(bf16[768,768]{1,0:T(8,128)(2,1)S(1)} %pad_maximum_fusion.1), channel_id=1, source_target_pairs={{0,1},{1,0},{2,3},{3,2},{4,5},{5,4},{6,7},{7,6},{8,9},{9,8},{10,11... | collective-permute-start | bytes 3538952 | tf_op jit(solution)/shard_map/ppermute | solution.py:35
  62.8 12.5 %collective-permute-start.3 = (bf16[128,3840]{1,0:T(8,128)(2,1)S(1)}, bf16[128,3840]{1,0:T(8,128)(2,1)S(1)}, u32[]{:S(2)}, u32[]{:S(2)}) collective-permute-start(bf16[128,3840]{1,0:T(8,128)(2,1)S(1)} %collective-permute-done.2.refs_8_), channel_id=1, source_target_pairs={{0,1},{1,0},{2,3},{3,2},{4,5},{5,4},{6,7},{7,6},{8,9},{9,8},{10,11... | collective-permute-start | bytes 2949128 | tf_op jit(solution)/shard_map/ppermute | solution.py:35
  63.3 12.9 %collective-permute-start.1 = (bf16[128,3840]{1,0:T(8,128)(2,1)}, bf16[128,3840]{1,0:T(8,128)(2,1)}, u32[]{:S(2)}, u32[]{:S(2)}) collective-permute-start(bf16[128,3840]{1,0:T(8,128)(2,1)} %collective-permute-done.refs_6_), channel_id=1, source_target_pairs={{0,1},{1,0},{2,3},{3,2},{4,5},{5,4},{6,7},{7,6},{8,9},{9,8},{10,11... | collective-permute-start | bytes 2949128 | tf_op jit(solution)/shard_map/ppermute | solution.py:35
  64.5 7.2 %collective-permute-start.8 = (bf16[128,768]{1,0:T(8,128)(2,1)S(1)}, bf16[128,768]{1,0:T(8,128)(2,1)S(1)}, u32[]{:S(2)}, u32[]{:S(2)}) collective-permute-start(bf16[128,768]{1,0:T(8,128)(2,1)S(1)} %copy-done.18), channel_id=1, source_target_pairs={{0,4},{4,0},{1,5},{5,1},{2,6},{6,2},{3,7},{7,3},{8,12},{12,8},{9,1... | collective-permute-start | bytes 589832 | tf_op jit(solution)/shard_map/ppermute | solution.py:35
  69.1 4.2 %collective-permute-start.6 = (bf16[128,1536]{1,0:T(8,128)(2,1)S(1)}, bf16[128,1536]{1,0:T(8,128)(2,1)S(1)}, u32[]{:S(2)}, u32[]{:S(2)}) collective-permute-start(bf16[128,1536]{1,0:T(8,128)(2,1)S(1)} %collective-permute-done.5.refs_11_), channel_id=1, source_target_pairs={{0,1},{1,0},{2,3},{3,2},{4,5},{5,4},{6,7},{7,6},{8,9},{9,8},{10,11... | collective-permute-start | bytes 1179656 | tf_op jit(solution)/shard_map/ppermute | solution.py:35
  73.2 2.2 %collective-permute-start.13 = (bf16[64,3840]{1,0:T(8,128)(2,1)}, bf16[64,3840]{1,0:T(8,128)(2,1)}, u32[]{:S(2)}, u32[]{:S(2)}) collective-permute-start(bf16[64,3840]{1,0:T(8,128)(2,1)} %collective-permute-done.11.refs_16_), channel_id=1, source_target_pairs={{0,1},{1,0},{2,3},{3,2},{4,5},{5,4},{6,7},{7,6},{8,9},{9,8},{10,11... | collective-permute-start | bytes 1474568 | tf_op jit(solution)/shard_map/ppermute | solution.py:35
  74.0 2.2 %collective-permute-start.12 = (bf16[64,3840]{1,0:T(8,128)(2,1)}, bf16[64,3840]{1,0:T(8,128)(2,1)}, u32[]{:S(2)}, u32[]{:S(2)}) collective-permute-start(bf16[64,3840]{1,0:T(8,128)(2,1)} %collective-permute-done.10.refs_15_), channel_id=1, source_target_pairs={{0,1},{1,0},{2,3},{3,2},{4,5},{5,4},{6,7},{7,6},{8,9},{9,8},{10,11... | collective-permute-start | bytes 1474568 | tf_op jit(solution)/shard_map/ppermute | solution.py:35
  94.2 4.5 %collective-permute-start.22 = (f32[8,128]{1,0:T(8,128)S(1)}, f32[8,128]{1,0:T(8,128)S(1)}, u32[]{:S(2)}, u32[]{:S(2)}) collective-permute-start(f32[8,128]{1,0:T(8,128)S(1)} %add.126.refs_0_), channel_id=1, source_target_pairs={{0,6},{2,4},{4,2},{6,0},{1,7},{3,5},{5,3},{7,1},{8,14},{10,12},{12... | collective-permute-start | bytes 12296 | tf_op jit(solution)/shard_map/ppermute | solution.py:35
  96.7 3.6 %collective-permute-start.21 = (f32[8,128]{1,0:T(8,128)S(1)}, f32[8,128]{1,0:T(8,128)S(1)}, u32[]{:S(2)}, u32[]{:S(2)}) collective-permute-start(f32[8,128]{1,0:T(8,128)S(1)} %add.126.refs_0_), channel_id=1, source_target_pairs={{0,2},{2,0},{1,3},{3,1},{4,6},{6,4},{5,7},{7,5},{8,10},{10,8},{9,1... | collective-permute-start | bytes 12296 | tf_op jit(solution)/shard_map/ppermute | solution.py:35
  97.1 3.6 %collective-permute-start.20 = (f32[8,128]{1,0:T(8,128)S(1)}, f32[8,128]{1,0:T(8,128)S(1)}, u32[]{:S(2)}, u32[]{:S(2)}) collective-permute-start(f32[8,128]{1,0:T(8,128)S(1)} %add.126.refs_0_), channel_id=1, source_target_pairs={{0,4},{4,0},{1,5},{5,1},{2,6},{6,2},{3,7},{7,3},{8,12},{12,8},{9,1... | collective-permute-start | bytes 12296 | tf_op jit(solution)/shard_map/ppermute | solution.py:35
  104.2 27.4 %collective-permute-start.28 = (bf16[784,384]{1,0:T(8,128)(2,1)}, bf16[784,384]{1,0:T(8,128)(2,1)S(1)}, u32[]{:S(2)}, u32[]{:S(2)}) collective-permute-start(bf16[784,384]{1,0:T(8,128)(2,1)} %get-tuple-element.56), channel_id=1, source_target_pairs={{0,136},{8,128},{128,8},{136,0},{1,137},{9,129},{129,9},{137,1},{2... | collective-permute-start | bytes 1806344 | tf_op jit(solution)/shard_map/ppermute | solution.py:35
  107.2 28.4 %collective-permute-start.27 = (bf16[784,384]{1,0:T(8,128)(2,1)}, bf16[784,384]{1,0:T(8,128)(2,1)S(1)}, u32[]{:S(2)}, u32[]{:S(2)}) collective-permute-start(bf16[784,384]{1,0:T(8,128)(2,1)} %get-tuple-element.57), channel_id=1, source_target_pairs={{0,128},{128,0},{1,129},{129,1},{2,130},{130,2},{3,131},{131,3},{4... | collective-permute-start | bytes 1806344 | tf_op jit(solution)/shard_map/ppermute | solution.py:35
  108.3 27.3 %collective-permute-start.26 = (bf16[784,384]{1,0:T(8,128)(2,1)}, bf16[784,384]{1,0:T(8,128)(2,1)S(1)}, u32[]{:S(2)}, u32[]{:S(2)}) collective-permute-start(bf16[784,384]{1,0:T(8,128)(2,1)} %get-tuple-element.58), channel_id=1, source_target_pairs={{0,8},{8,0},{1,9},{9,1},{2,10},{10,2},{3,11},{11,3},{4,12},{12,4},... | collective-permute-start | bytes 1806344 | tf_op jit(solution)/shard_map/ppermute | solution.py:35
  112.6 3.7 %collective-permute-start.23 = (f32[]{:T(128)}, f32[]{:T(128)}, u32[]{:S(2)}, u32[]{:S(2)}) collective-permute-start(f32[]{:T(128)} %select_n.85), channel_id=1, source_target_pairs={{0,16},{16,0},{32,48},{48,32},{64,80},{80,64},{96,112},{112,96},{1... | collective-permute-start | bytes 20 | tf_op jit(solution)/shard_map/ppermute | solution.py:356
  116.9 5.0 %collective-permute-start.24 = (f32[]{:T(128)}, f32[]{:T(128)}, u32[]{:S(2)}, u32[]{:S(2)}) collective-permute-start(f32[]{:T(128)} %add.128), channel_id=1, source_target_pairs={{0,32},{16,48},{32,0},{48,16},{64,96},{80,112},{96,64},{112,80},{1... | collective-permute-start | bytes 20 | tf_op jit(solution)/shard_map/ppermute | solution.py:356
  122.4 8.6 %collective-permute-start.25 = (f32[]{:T(128)}, f32[]{:T(128)}, u32[]{:S(2)}, u32[]{:S(2)}) collective-permute-start(f32[]{:T(128)} %add.129), channel_id=1, source_target_pairs={{0,64},{16,80},{32,96},{48,112},{64,0},{80,16},{96,32},{112,48},{1... | collective-permute-start | bytes 20 | tf_op jit(solution)/shard_map/ppermute | solution.py:356
  139.2 27.9 %all-to-all-start = ((bf16[16,48,384]{2,1,0:T(8,128)(2,1)}), bf16[16,48,384]{2,1,0:T(8,128)(2,1)S(1)}, u32[]{:S(2)}, u32[]{:S(2)}) async-start(bf16[16,48,384]{2,1,0:T(8,128)(2,1)} %bitcast.24), calls=%async_computation | async-start | bytes 1179648 | tf_op jit(solution)/shard_map/all_to_all | solution.py:363
  149.3 12.6 %collective-permute-start.31 = (f32[]{:T(128)}, f32[]{:T(128)}, u32[]{:S(2)}, u32[]{:S(2)}) collective-permute-start(f32[]{:T(128)} %add.130), channel_id=1, source_target_pairs={{0,136},{8,128},{128,8},{136,0},{1,137},{9,129},{129,9},{137,1},{2... | collective-permute-start | bytes 20 | tf_op jit(solution)/shard_map/ppermute | solution.py:35
  153.8 8.1 %collective-permute-start.30 = (f32[]{:T(128)}, f32[]{:T(128)}, u32[]{:S(2)}, u32[]{:S(2)}) collective-permute-start(f32[]{:T(128)} %add.130), channel_id=1, source_target_pairs={{0,128},{128,0},{1,129},{129,1},{2,130},{130,2},{3,131},{131,3},{4... | collective-permute-start | bytes 20 | tf_op jit(solution)/shard_map/ppermute | solution.py:35
  156.2 5.2 %collective-permute-start.29 = (f32[]{:T(128)}, f32[]{:T(128)}, u32[]{:S(2)}, u32[]{:S(2)}) collective-permute-start(f32[]{:T(128)} %add.130), channel_id=1, source_target_pairs={{0,8},{8,0},{1,9},{9,1},{2,10},{10,2},{3,11},{11,3},{4,12},{12,4},... | collective-permute-start | bytes 20 | tf_op jit(solution)/shard_map/ppermute | solution.py:35
  (23 other events, 165.2 us)
Sparse Core Ops, SparseCore 0:
  26.3 43.5 all-gather.1
